TPU v7x, 256 devices: a whole 4x4x8 slice. The times are simulated.
256 devices in a mesh: tiles: 32 (over z, y), fft: 8 (over x, core).
Axes of the slice: x: 4, y: 4, z: 8, core: 2. Of those that a mesh axis runs over, the one named last changes fastest.
Arguments:
- cotangent: bfloat16 [65536, 4096], P(('tiles', 'fft')), may hold values from -6 to 6
- base_grad: bfloat16 [65536, 4096], P(('tiles', 'fft')), may hold values from -6 to 6
- tile_place: int32 [65536], P(('tiles', 'fft')), may hold values from 0 to 1048575, as said below
- tile_count: int32 [256], P(('tiles', 'fft')), may hold values from 64 to 256, as said below
- psf_spectrum: float32 [2, 1536, 2048], P(None, None, 'fft'), may hold values from -2.4 to 2.4
Outputs:
- mask_grad: bfloat16 [65536, 4096], P(('tiles', 'fft'))
Inputs may be any that keep to these rules, and one draw needn't show every extreme that they name: `tile_place`: slots form groups of 256; the live slots of group q hold distinct tiles whose tile row lies in band q mod 8 (tile rows (q mod 8) * 16 up to the next band); at most 8 live tiles of one group lie in one block of 1024 columns, and some group reaches that; no tile appears in two slots; slots past the count hold 0. `tile_count`: some group of every band is full.
All inputs are finite; a program needn't handle non-finite values.
Results may differ from a plain program's by a relative error of at most 0.001.
Values sent between devices are 32-bit elements; how exact they have to be, the bound alone decides.
No kernel may reach another device: no remote copies, remote signals or barrier semaphores. Data moves between devices by JAX's collectives and lax.ppermute only.
A program may use at most 192 MiB of HBM per device.

v0:
```python
import math

import jax
import jax.numpy as jnp
from jax import lax
from jax.sharding import PartitionSpec as P

ROWS_DEV = 64
BLOCK = 1024
REACH = 512
SUB = 16
TCELL = 4
BUCKET = 8


def with_halo(block, sides, width):
    for axis, dim in sides:
        count = lax.axis_size(axis)
        forward = [(i, i + 1) for i in range(count - 1)]
        backward = [(target, source) for source, target in forward]
        low = lax.ppermute(
            lax.slice_in_dim(block, block.shape[dim] - width, None, axis=dim), axis, forward
        )
        high = lax.ppermute(lax.slice_in_dim(block, 0, width, axis=dim), axis, backward)
        block = jnp.concatenate([low, block, high], axis=dim)
    return block


def phase_table(inputs, outputs, shift_out, length):
    rows_axis = jnp.arange(inputs, dtype=jnp.int32)[:, None]
    cols_axis = jnp.arange(outputs, dtype=jnp.int32)[None, :] + shift_out
    angles = (rows_axis * cols_axis % length).astype(jnp.float32) * (2.0 * math.pi / length)
    return (jnp.cos(angles), jnp.sin(angles))


def product(left, right):
    return jnp.dot(left, right, precision=lax.Precision.HIGHEST, preferred_element_type=jnp.float32)


def local(cotangent, base_grad, tile_place, tile_count, psf_spectrum):
    holders = lax.axis_size("tiles")
    band_index = lax.axis_index("fft")
    slot_total = tile_place.shape[0]
    cell_count = TCELL * TCELL
    tile_cols = BLOCK // TCELL
    tile_rows = ROWS_DEV // TCELL
    spot_total = tile_rows * tile_cols
    length_cols = BLOCK + 2 * REACH
    length_rows = psf_spectrum.shape[1]
    active = jnp.arange(slot_total, dtype=jnp.int32) < tile_count[0]
    row_tile = tile_place // (holders * tile_cols)
    col_tile = tile_place % (holders * tile_cols)
    target = col_tile // tile_cols
    position = (row_tile - band_index * tile_rows) * tile_cols + col_tile % tile_cols
    pooled = jnp.sum(
        cotangent.reshape(slot_total, TCELL, SUB, TCELL, SUB), axis=(2, 4), dtype=jnp.float32
    )
    pooled = pooled.reshape(slot_total, cell_count)
    member = (target[:, None] == jnp.arange(holders, dtype=jnp.int32)[None, :]) & active[:, None]
    member_int = member.astype(jnp.int32)
    bucket_rank = jnp.sum((jnp.cumsum(member_int, axis=0) - member_int) * member_int, axis=1)
    bucket_slot = jnp.where(active, target * BUCKET + bucket_rank, holders * BUCKET)
    sending = (
        jnp.zeros((holders * BUCKET + 1, cell_count), jnp.float32).at[bucket_slot].set(pooled)[:-1]
    )
    sent_marks = (
        jnp.zeros((holders * BUCKET + 1,), jnp.float32)
        .at[bucket_slot]
        .set((position + 1).astype(jnp.float32))[:-1]
    )
    arrived, arrival_marks = (
        lax.all_to_all(
            sending.reshape(holders, BUCKET, cell_count),
            "tiles",
            split_axis=0,
            concat_axis=0,
            tiled=True,
        ),
        lax.all_to_all(
            sent_marks.reshape(holders, BUCKET), "tiles", split_axis=0, concat_axis=0, tiled=True
        ),
    )
    arrival_spot = arrival_marks.reshape(-1).astype(jnp.int32) - 1
    scatter_spot = jnp.where(arrival_spot >= 0, arrival_spot, spot_total)
    coarse_grid = (
        jnp.zeros((spot_total + 1, cell_count), jnp.float32)
        .at[scatter_spot]
        .add(arrived.reshape(-1, cell_count))[:-1]
    )
    coarse_map = (
        coarse_grid.reshape(tile_rows, tile_cols, TCELL, TCELL)
        .transpose(0, 2, 1, 3)
        .reshape(ROWS_DEV, BLOCK)
    )
    extended = with_halo(coarse_map, (("tiles", 1),), REACH)
    cos_cols, sin_cols = phase_table(length_cols, length_cols, 0, length_cols)
    forward_real = product(extended, cos_cols)
    forward_imag = -product(extended, sin_cols)
    columns = lax.all_to_all(
        jnp.stack([forward_real, forward_imag]), "fft", split_axis=2, concat_axis=1, tiled=True
    )
    strip_rows = columns.shape[1]
    cos_rows, sin_rows = phase_table(length_rows, strip_rows, REACH, length_rows)
    spec_real = product(cos_rows, columns[0]) + product(sin_rows, columns[1])
    spec_imag = product(cos_rows, columns[1]) - product(sin_rows, columns[0])
    mixed_real = spec_real * psf_spectrum[0] - spec_imag * psf_spectrum[1]
    mixed_imag = spec_real * psf_spectrum[1] + spec_imag * psf_spectrum[0]
    back_real = (product(cos_rows.T, mixed_real) - product(sin_rows.T, mixed_imag)) / length_rows
    back_imag = (product(cos_rows.T, mixed_imag) + product(sin_rows.T, mixed_real)) / length_rows
    returned = lax.all_to_all(
        jnp.stack([back_real, back_imag]), "fft", split_axis=1, concat_axis=2, tiled=True
    )
    cos_back, sin_back = phase_table(length_cols, BLOCK, REACH, length_cols)
    sensitivity = (product(returned[0], cos_back) - product(returned[1], sin_back)) / length_cols
    sens_patch = (
        sensitivity.reshape(tile_rows, TCELL, tile_cols, TCELL)
        .transpose(0, 2, 1, 3)
        .reshape(spot_total, cell_count)
    )
    wanted = target * spot_total + position
    piece = lax.all_gather(sens_patch, "tiles", axis=0, tiled=True)
    inside = (wanted >= 0) & (wanted < piece.shape[0]) & active
    fetched = jnp.take(piece, jnp.clip(wanted, 0, piece.shape[0] - 1), axis=0)
    mine = jnp.where(inside[:, None], fetched, 0.0)
    upsampled = jnp.broadcast_to(
        mine.reshape(slot_total, TCELL, 1, TCELL, 1), (slot_total, TCELL, SUB, TCELL, SUB)
    )
    upsampled = upsampled.reshape(slot_total, TCELL * SUB * TCELL * SUB)
    return (base_grad.astype(jnp.float32) + upsampled).astype(jnp.bfloat16)


def solution(mesh):
    return jax.shard_map(
        local,
        mesh=mesh,
        in_specs=(
            P(("tiles", "fft"), None),
            P(("tiles", "fft"), None),
            P(("tiles", "fft")),
            P(("tiles", "fft")),
            P(None, None, "fft"),
        ),
        out_specs=P(("tiles", "fft"), None),
        check_vma=False,
    )
```

profile of v0, /device:TPU:1, one launch (start us, length us, event | category | flops | bytes accessed | tf_op | source)
XLA Modules:
  0.0 942.5 jit_solution(14469455189208089812)
XLA Ops:
  7.2 0.7 and_and_fusion
  8.9 1.4 scatter_custom_fusion
  10.3 0.7 all_to_all.31
  11.0 12.0 %all-to-all-start = ((f32[32,1,8]{2,1,0:T(1,128)}), f32[32,1,8]{2,1,0:T(1,128)S(1)}, u32[]{:S(2)}, u32[]{:S(2)}) async-start(f32[32,1,8]{2,1,0:T(1,128)} %bitcast.3), calls=%async_computation | async-start | bytes 32768 | tf_op jit(solution)/shard_map/all_to_all | solution.py:79
  23.0 3.3 copy.46
  26.8 1.2 scatter_custom_fusion.1
  28.0 0.7 reshape.190
  28.7 2.8 all-to-all-done
  31.5 6.4 all-to-all-start.1
  38.1 8.4 all-to-all-done.1
  47.7 2.1 scatter_custom_fusion.2
  49.8 1.5 slice.64
  51.3 2.2 copy.48
  53.5 4.7 copy.49
  58.2 8.4 reshape.136
  66.6 2.2 collective-permute-start
  68.8 1.5 collective-permute-start.1
  70.8 3.7 collective-permute-done.1
  74.5 70.7 %fusion.54 = f32[1,64,2048]{2,1,0:T(8,128)S(1)} fusion(f32[64,2048]{1,0:T(8,128)S(1)} %constant_dynamic-update-slice_fusion), kind=kOutput, calls=%fused_computation.52 | convolution fusion | flops 3279945728 | bytes 1048576 | tf_op jit(solution)/shard_map/dot_general | solution.py:37
  145.3 71.7 %fusion.60 = f32[1,64,2048]{2,1,0:T(8,128)S(1)} fusion(f32[64,2048]{1,0:T(8,128)S(1)} %constant_dynamic-update-slice_fusion), kind=kOutput, calls=%fused_computation.54 | convolution fusion | flops 3280076800 | bytes 1048576 | tf_op jit(solution)/shard_map/dot_general | solution.py:37
  217.1 1.1 copy.50
  218.1 3.0 reshape.192
  221.2 8.4 all-to-all-start.2
  229.5 15.1 %all-to-all-done.2 = f32[8,1,32768]{2,1,0:T(1,128)S(1)} async-done(((f32[8,1,32768]{2,1,0:T(1,128)}), f32[8,1,32768]{2,1,0:T(1,128)S(1)}, u32[]{:S(2)}, u32[]{:S(2)}) %all-to-all-start.2) | async-done | bytes 1048608 | tf_op jit(solution)/shard_map/all_to_all | solution.py:99
  244.6 3.1 reduce.7
  247.7 1.5 reshape.193
  249.2 1.1 copy.60
  250.7 14.6 %fusion.37 = f32[1536,256]{1,0:T(8,128)S(1)} fusion(f32[512,256]{1,0:T(8,128)S(1)} %bitcast.123, s32[512]{0:T(512)S(1)} %iota_add_fusion.1), kind=kOutput, calls=%fused_computation.44 | convolution fusion | flops 2422996992 | bytes 2099200 | tf_op jit(solution)/shard_map/dot_general | solution.py:37
  265.3 14.7 %fusion.35 = f32[1536,256]{1,0:T(8,128)S(1)} fusion(f32[512,256]{1,0:T(8,128)S(1)} %bitcast.127, s32[512]{0:T(512)S(1)} %iota_add_fusion.1), kind=kOutput, calls=%fused_computation.43 | convolution fusion | flops 2422996992 | bytes 2099200 | tf_op jit(solution)/shard_map/dot_general | solution.py:37
  280.0 14.6 %fusion.48 = f32[1536,256]{1,0:T(8,128)S(1)} fusion(f32[1536,256]{1,0:T(8,128)S(1)} %fusion.37, f32[512,256]{1,0:T(8,128)S(1)} %bitcast.128, s32[512]{0:T(512)S(1)} %iota_add_fusion.1), kind=kOutput, calls=%fused_computation.50 | convolution fusion | flops 2423390208 | bytes 3672064 | tf_op jit(solution)/shard_map/dot_general | solution.py:37
  294.6 15.3 %fusion.63 = (f32[1536,256]{1,0:T(8,128)S(1)}, f32[1536,256]{1,0:T(8,128)S(1)}) fusion(f32[1536,256]{1,0:T(8,128)S(1)} %fusion.48, f32[2,1536,256]{2,1,0:T(8,128)S(1)} %copy-done, f32[1536,256]{1,0:T(8,128)S(1)} %fusion.35, f32[512,256]{1,0:T(8,128)S(1)} %bitcast.124, s32[512]{0:T(512)S(1)} %iota_add_fusion.1), kind=kOutput, calls=%fused_computation.57 | convolution fusion | flops 2425749504 | bytes 9963520 | tf_op jit(solution)/shard_map/dot_general | solution.py:37
  310.0 17.6 %fusion.33 = f32[512,256]{1,0:T(8,128)S(1)} fusion(f32[1536,256]{1,0:T(8,128)S(1)} %get-tuple-element.10, s32[512]{0:T(512)S(1)} %iota_add_fusion.1), kind=kOutput, calls=%fused_computation.42 | convolution fusion | flops 2422996992 | bytes 2099200 | tf_op jit(solution)/shard_map/dot_general | solution.py:37
  327.6 17.6 %fusion.31 = f32[512,256]{1,0:T(8,128)S(1)} fusion(f32[1536,256]{1,0:T(8,128)S(1)} %get-tuple-element.11, s32[512]{0:T(512)S(1)} %iota_add_fusion.1), kind=kOutput, calls=%fused_computation.41 | convolution fusion | flops 2422996992 | bytes 2099200 | tf_op jit(solution)/shard_map/dot_general | solution.py:37
  345.1 17.9 %fusion.103 = f32[1,512,256]{2,1,0:T(8,128)S(1)} fusion(f32[512,256]{1,0:T(8,128)S(1)} %fusion.33, f32[1536,256]{1,0:T(8,128)S(1)} %get-tuple-element.11, s32[512]{0:T(512)S(1)} %iota_add_fusion.1), kind=kOutput, calls=%fused_computation.87 | convolution fusion | flops 2423259136 | bytes 2623488 | tf_op jit(solution)/shard_map/dot_general | solution.py:37
  363.0 17.7 %fusion.112 = f32[1,512,256]{2,1,0:T(8,128)S(1)} fusion(f32[512,256]{1,0:T(8,128)S(1)} %fusion.31, f32[1536,256]{1,0:T(8,128)S(1)} %get-tuple-element.10, s32[512]{0:T(512)S(1)} %iota_add_fusion.1), kind=kOutput, calls=%fused_computation.90 | convolution fusion | flops 2423259136 | bytes 2623488 | tf_op jit(solution)/shard_map/dot_general | solution.py:37
  380.9 1.8 copy.54
  382.6 4.3 all-to-all-start.3
  387.0 15.1 %all-to-all-done.3 = f32[2,512,256]{2,0,1:T(2,128)S(1)} async-done(((f32[2,512,256]{2,0,1:T(2,128)}), f32[2,512,256]{2,0,1:T(2,128)S(1)}, u32[]{:S(2)}, u32[]{:S(2)}) %all-to-all-start.3) | async-done | bytes 1048608 | tf_op jit(solution)/shard_map/all_to_all | solution.py:110
  403.1 35.8 %fusion.13 = f32[64,1024]{1,0:T(8,128)S(1)} fusion(f32[64,2048]{1,0:T(8,128)S(1)} %bitcast.125, s32[1024]{0:T(1024)S(1)} %iota_add_fusion), kind=kOutput, calls=%fused_computation.23 | convolution fusion | flops 1639972864 | bytes 790528 | tf_op jit(solution)/shard_map/dot_general | solution.py:37
  438.9 35.6 %fusion.118 = f32[64,1024]{1,0:T(8,128)S(1)} fusion(f32[64,1024]{1,0:T(8,128)S(1)} %fusion.13, f32[64,2048]{1,0:T(8,128)S(1)} %bitcast.126, s32[1024]{0:T(1024)S(1)} %iota_add_fusion), kind=kOutput, calls=%fused_computation.92 | convolution fusion | flops 1640103936 | bytes 1052672 | tf_op jit(solution)/shard_map/dot_general | solution.py:37
  474.6 10.0 %reshape.137 = f32[16,4,256,4]{3,2,1,0:T(8,128)} reshape(f32[64,1024]{1,0:T(8,128)S(1)} %fusion.118) | data formatting | bytes 524288 | tf_op jit(solution)/shard_map/reshape | solution.py:116
  484.6 5.2 copy.56
  490.0 1.9 copy.57
  492.0 3.3 copy.43
  495.3 425.5 %all-gather.2.cloned.1.call-done = f32[131072,16]{1,0:T(8,128)} async-done(((f32[4096,16]{1,0:T(8,128)}), f32[131072,16]{1,0:T(8,128)}) %all-gather.2.cloned.1.call-update) | async-done | bytes 8388624 | tf_op jit(solution)/shard_map/all_gather | solution.py:121
  920.8 8.4 gather_fusion
  929.3 1.8 fusion.22
  931.1 4.1 copy.59
  (47 shorter events, 5.2 us)
Async XLA Ops:
  11.0 20.5 %all-to-all-start = ((f32[32,1,8]{2,1,0:T(1,128)}), f32[32,1,8]{2,1,0:T(1,128)S(1)}, u32[]{:S(2)}, u32[]{:S(2)}) async-start(f32[32,1,8]{2,1,0:T(1,128)} %bitcast.3), calls=%async_computation | async-start | bytes 32768 | tf_op jit(solution)/shard_map/all_to_all | solution.py:79
  31.5 15.0 %all-to-all-start.1 = ((f32[32,1,128]{2,1,0:T(1,128)}), f32[32,1,128]{2,1,0:T(1,128)S(1)}, u32[]{:S(2)}, u32[]{:S(2)}) async-start(f32[32,1,128]{2,1,0:T(1,128)} %reshape.190), calls=%async_computation.1 | async-start | bytes 32768 | tf_op jit(solution)/shard_map/all_to_all | solution.py:72
  66.6 4.1 collective-permute-start
  68.8 5.7 collective-permute-start.1
  221.2 23.5 %all-to-all-start.2 = ((f32[8,1,32768]{2,1,0:T(1,128)}), f32[8,1,32768]{2,1,0:T(1,128)S(1)}, u32[]{:S(2)}, u32[]{:S(2)}) async-start(f32[8,1,32768]{2,1,0:T(1,128)} %reshape.192), calls=%async_computation.2 | async-start | bytes 2097152 | tf_op jit(solution)/shard_map/all_to_all | solution.py:99
  280.0 14.6 %copy-start = (f32[2,1536,256]{2,1,0:T(8,128)S(1)}, f32[2,1536,256]{2,1,0:T(8,128)}, u32[]{:S(2)}) copy-start(f32[2,1536,256]{2,1,0:T(8,128)} %param.9) | copy-start | bytes 9437188
  382.6 19.4 %all-to-all-start.3 = ((f32[2,512,256]{2,0,1:T(2,128)}), f32[2,512,256]{2,0,1:T(2,128)S(1)}, u32[]{:S(2)}, u32[]{:S(2)}) async-start(f32[2,512,256]{2,0,1:T(2,128)} %copy.54), calls=%async_computation.3 | async-start | bytes 2097152 | tf_op jit(solution)/shard_map/all_to_all | solution.py:110
  387.0 533.8 %all-gather.2.cloned.1.call-start = ((), (), s32[]{:S(2)}) async-start(), calls=%async_computation.4 | async-start | bytes 69206016 | tf_op jit(solution)/shard_map/all_gather | solution.py:121
Sparse Core Ops, SparseCore 0:
  492.1 428.6 all-gather.1
where the time goes:
time: 949 us; the launch traced here: 942 us
  waiting for transfers between devices  471 us (50%)
  matrix products  344 us (36%)
  local copies, waits for them, and re-layouts  68.1 us (7%)
  starting transfers between devices  34.8 us (4%)
  between operations  14.9 us (2%)
  other arithmetic  9.66 us (1%)
    all_gather x1, waiting for transfers between devices, local(): piece = lax.all_gather(sens_patch, 'tiles', axis=0, tiled=True)  426 us
    dot_general x12, matrix products, product(): jnp.dot(left, right, precision=lax.Precision.HIGHEST, preferred_element_t...  344 us
  transfers between devices with their start and end apart: 7, of which 7 were waited for; matrix products, arithmetic and copies ran while one was open for 1% of the time, Pallas kernels for 0%

commit v1 on v0

v1 whole, which is shorter than its diff:
```python
import functools
import math

import jax
import jax.numpy as jnp
import ml_dtypes
import numpy as np
from jax import lax
from jax.experimental import pallas as pl
from jax.experimental.pallas import tpu as pltpu
from jax.sharding import PartitionSpec as P

BANDS = 8
BLOCKS = 32
BUCKET = 8
SLOTS = 256
SUB = 16
TCELL = 4
CELLS = 16
TILE_ROWS = 16
TILE_COLS = 256
ROWS = 512
L0 = 1536
L1 = 2048
STRIP = 256
HALF = 128
PART0 = L0 // 4
WIDE = 512
BF = jnp.bfloat16
F32 = jnp.float32
VMEM_LIMIT = 52 * 1024 * 1024


def split_np(table):
    high = table.astype(ml_dtypes.bfloat16)
    low = (table - high.astype(np.float64)).astype(ml_dtypes.bfloat16)
    return high, low


@functools.lru_cache(maxsize=None)
def tables():
    k = np.arange(L1)
    u = np.arange(L1 // 2).reshape(256, 4).T.reshape(-1)
    angle = (np.outer(2 * u + 1, k) % (2 * L1)) * (math.pi / L1)
    cos, sin = np.cos(angle), np.sin(angle)

    def strips(table):
        return table.reshape(table.shape[0], BANDS, STRIP).transpose(1, 0, 2)

    ch, cl = split_np(strips(cos))
    sh, sl = split_np(strips(-sin))
    fwd = np.stack([ch, cl, sh, sl], axis=1)
    near = (u < 2 * STRIP)
    scale = 1.0 / (L0 * L1)
    ch, cl = split_np(strips(cos[near]).transpose(0, 2, 1) * scale)
    sh, sl = split_np(strips(sin[near]).transpose(0, 2, 1) * scale)
    back = np.stack([ch, cl, sh, sl], axis=1)
    k0 = np.arange(PART0)
    rows = []
    for i in range(4):
        angle = (np.outer(k0, 4 * np.arange(128) + i) % L0) * (2 * math.pi / L0)
        c, s = np.cos(angle), np.sin(angle)
        rows.append(np.block([[c, s], [-s, c]]))
    rows = np.stack(rows)
    rfwd = np.stack(split_np(rows))
    rback = np.stack(split_np(rows.transpose(0, 2, 1)))
    return fwd, back, rfwd, rback


def split(x):
    high = x.astype(BF)
    low = (x - high.astype(F32)).astype(BF)
    return high, low


def split3(x):
    high = x.astype(BF)
    rest = x - high.astype(F32)
    mid = rest.astype(BF)
    low = (rest - mid.astype(F32)).astype(BF)
    return high, mid, low


def dot(a, b):
    return jnp.dot(a, b, preferred_element_type=F32)


def dot_nt(a, b):
    return lax.dot_general(a, b, (((1,), (1,)), ((), ())), preferred_element_type=F32)


def iota(shape, dim):
    return lax.broadcasted_iota(jnp.int32, shape, dim)


def pool_kernel(count_ref, place_ref, cot_hbm, msg_ref, meta_ref, cot, sems):
    copies = [
        pltpu.make_async_copy(
            cot_hbm.at[:, pl.ds(i * 1024, 1024)], cot.at[:, pl.ds(i * 1024, 1024)], sems.at[i]
        )
        for i in range(4)
    ]
    for copy in copies:
        copy.start()
    count = count_ref[0]
    place_row = place_ref[...]
    square = (SLOTS, SLOTS)
    down, across = iota(square, 0), iota(square, 1)

    def fields(place, live):
        column = place & (BLOCKS * TILE_COLS - 1)
        row = (place >> 13) & (TILE_ROWS - 1)
        target = jnp.where(live, column >> 8, -8)
        return row, target, column & (TILE_COLS - 1)

    live_row = iota((1, SLOTS), 1) < count
    _, target_row, tc_row = fields(place_row, live_row)
    place_col = jnp.sum(
        jnp.where(down == across, place_row.astype(F32), 0.0), axis=1, keepdims=True
    ).astype(jnp.int32)
    live_col = iota((SLOTS, 1), 0) < count
    tr_col, target_col, tc_col = fields(place_col, live_col)
    before = (target_row == target_col) & (across < down) & live_row
    rank_col = jnp.sum(jnp.where(before, 1.0, 0.0), axis=1, keepdims=True).astype(jnp.int32)
    right_col = tc_col >= HALF
    lane = iota((SLOTS, 128), 1)
    meta_ref[...] = jnp.where(
        lane == 0, target_col, jnp.where(lane == 1, rank_col, right_col.astype(jnp.int32))
    )
    b = iota((BLOCKS, SLOTS), 0)
    right_row = tc_row >= HALF
    hot_own = target_row == b
    hot_left = (target_row == b - 1) & right_row & live_row
    hot_right = (target_row == b + 1) & (~right_row) & live_row
    hot = jnp.concatenate(
        [jnp.where(h, 1.0, 0.0) for h in (hot_own, hot_left, hot_right)], axis=0
    ).astype(BF)
    code_own = 1 + tr_col * 256 + jnp.where(right_col, tc_col - HALF, 255 - tc_col)
    code_halo = 1 + tr_col * 256 + jnp.where(right_col, 255 - tc_col, tc_col)
    mark_own = jnp.where(lane == rank_col, code_own, 0).astype(F32)
    mark_halo = jnp.where((lane & 7) == rank_col, code_halo, 0).astype(F32)
    prow, plane = iota((256, 256), 0), iota((256, 256), 1)
    want_j = (plane >> 2) & 3
    want_j = jnp.where(plane >= 128, 3 - want_j, want_j)
    match_j = ((prow >> 4) & 3) == want_j
    total = jnp.zeros((SLOTS, 256), F32)
    for i in range(4):
        weights = jnp.where(match_j & ((plane & 3) == i), 1.0, 0.0).astype(BF)
        copies[i].wait()
        for c in range(4):
            total = total + dot(cot[:, i * 1024 + c * 256 : i * 1024 + (c + 1) * 256], weights)
    plain, flipped = total[:, :128], total[:, 128:]
    here = (lane >> 4) == rank_col
    own = jnp.where(here, jnp.where(right_col, plain, flipped), 0.0)
    halo = jnp.where(here, jnp.where(right_col, flipped, plain), 0.0)
    loads = jnp.concatenate([own, halo, mark_own, mark_halo], axis=1)
    out = jnp.zeros((3 * BLOCKS, 512), F32)
    for piece in split3(loads):
        out = out + dot(hot, piece)
    lane32 = iota((BLOCKS, 128), 1)
    marks = jnp.where(
        lane32 < 8,
        out[0:32, 256:384],
        jnp.where(lane32 < 16, out[32:64, 384:512], jnp.where(lane32 < 24, out[64:96, 384:512], 0.0)),
    )
    message = jnp.concatenate(
        [out[0:32, 0:128], out[32:64, 128:256], out[64:96, 128:256], marks], axis=1
    )
    for f in range(BANDS):
        msg_ref[f * BLOCKS : (f + 1) * BLOCKS, :] = message


def pool(cotangent, tile_place, tile_count):
    return pl.pallas_call(
        pool_kernel,
        out_shape=(
            jax.ShapeDtypeStruct((BANDS * BLOCKS, WIDE), F32),
            jax.ShapeDtypeStruct((SLOTS, 128), jnp.int32),
        ),
        in_specs=[
            pl.BlockSpec(memory_space=pltpu.SMEM),
            pl.BlockSpec(memory_space=pltpu.VMEM),
            pl.BlockSpec(memory_space=pl.ANY),
        ],
        out_specs=(
            pl.BlockSpec(memory_space=pltpu.VMEM),
            pl.BlockSpec(memory_space=pltpu.VMEM),
        ),
        scratch_shapes=[pltpu.VMEM((SLOTS, 4096), BF), pltpu.SemaphoreType.DMA((4,))],
        compiler_params=pltpu.CompilerParams(vmem_limit_bytes=VMEM_LIMIT),
        name="pool",
    )(tile_count, tile_place.reshape(1, SLOTS), cotangent)


def chunk_swap(pieces, lane):
    out = []
    for band in range(4):
        value = None
        for e in range(4):
            moved = pieces[e] if e == band else pltpu.roll(pieces[e], ((e - band) * 32) % 128, 1)
            value = moved if value is None else jnp.where((lane >> 5) == e, moved, value)
        out.append(value)
    return out


def conv_kernel(
    f_ref, recv_ref, fwd_hbm, rfwd_hbm, psf_hbm, rback_hbm, back_hbm, out_ref,
    fwd, rfwd, psf, rback, back, tv, tm, e_s, o_s, y_s, q_s, s_s, tg, sems,
):
    f = f_ref[0, 0]
    copies = [
        pltpu.make_async_copy(fwd_hbm.at[f], fwd, sems.at[0]),
        pltpu.make_async_copy(rfwd_hbm, rfwd, sems.at[1]),
        pltpu.make_async_copy(psf_hbm, psf, sems.at[2]),
        pltpu.make_async_copy(rback_hbm, rback, sems.at[3]),
        pltpu.make_async_copy(back_hbm.at[f], back, sems.at[4]),
    ]
    for copy in copies:
        copy.start()

    turned = jnp.transpose(recv_ref[...])
    lane16 = iota((16, 128), 1)
    lane8 = iota((8, 128), 1)
    for nbr in range(3):
        for eh in range(2):
            for bh in range(2):
                group = [
                    turned[nbr * 128 + (eh * 4 + e) * 16 : nbr * 128 + (eh * 4 + e + 1) * 16,
                           bh * 128 : (bh + 1) * 128]
                    for e in range(4)
                ]
                for band, value in enumerate(chunk_swap(group, lane16)):
                    tv[bh * 4 + band, nbr, :, eh * 128 : (eh + 1) * 128] = value
                marks = turned[384 + nbr * 8 : 384 + nbr * 8 + 8, bh * 128 : (bh + 1) * 128]
                group = [
                    jnp.broadcast_to(marks[eh * 4 + e : eh * 4 + e + 1, :], (8, 128))
                    for e in range(4)
                ]
                for band, value in enumerate(chunk_swap(group, lane8)):
                    tm[bh * 4 + band, nbr, :, eh * 128 : (eh + 1) * 128] = (
                        value.astype(jnp.int32) - 1
                    )

    row16 = iota((16, 256), 0)

    def hot_of(code, rows):
        spot = jnp.broadcast_to(code[0:1, :] & 255, (rows, 256))
        return jnp.where(iota((rows, 256), 0) == spot, 1.0, 0.0).astype(BF)

    def scatter(band, carry):
        base = pl.multiple_of(band * 16, 16)
        outs = []
        for nbr in range(3):
            code = tm[band, nbr]
            mask = row16 == jnp.broadcast_to(code[0:1, :] >> 8, (16, 256))
            values = tv[band, nbr]
            high = values.astype(BF).astype(F32)
            low = values - high
            parts = []
            for piece in (high, low):
                for c in range(CELLS):
                    parts.append(
                        jnp.where(mask, jnp.broadcast_to(piece[c : c + 1, :], (16, 256)), 0.0).astype(BF)
                    )
            left = jnp.concatenate(parts, axis=0)
            both = dot_nt(left, hot_of(code, 256 if nbr == 0 else 128))
            outs.append(both[:256] + both[256:])
        near_r, near_l = outs[0][:, :128], outs[0][:, 128:]
        far_l, far_r = outs[1], outs[2]
        for ref, near, far in ((e_s, near_r + near_l, far_r + far_l), (o_s, near_r - near_l, far_r - far_l)):
            for part, value in enumerate((near, far)):
                for level, piece in enumerate(split(value)):
                    for j in range(4):
                        for i in range(4):
                            ref[level, pl.ds(i * 128 + base, 16),
                                j * 256 + part * 128 : j * 256 + (part + 1) * 128] = (
                                piece[(j * 4 + i) * 16 : (j * 4 + i + 1) * 16, :]
                            )
        return carry

    lax.fori_loop(0, BANDS, scatter, 0)

    copies[0].wait()
    for i in range(4):
        rows = slice(i * 128, (i + 1) * 128)
        for part, ref in enumerate((e_s, o_s)):
            high, low = ref[0, rows, :], ref[1, rows, :]
            table_high, table_low = fwd[2 * part], fwd[2 * part + 1]
            y = dot(high, table_high) + (dot(high, table_low) + dot(low, table_high))
            y_high, y_low = split(y)
            y_s[0, i, part * 128 : (part + 1) * 128, :] = y_high
            y_s[1, i, part * 128 : (part + 1) * 128, :] = y_low

    copies[1].wait()
    copies[2].wait()
    step = 64

    def middle(chunk, carry):
        start = pl.multiple_of(chunk * step, step)

        def row_part(i, part):
            rows = pl.ds(part * PART0 + start, step)
            high, low = rfwd[0, i, rows, :], rfwd[1, i, rows, :]
            return dot(high, y_s[0, i]) + (dot(high, y_s[1, i]) + dot(low, y_s[0, i]))

        g = [(row_part(i, 0), row_part(i, 1)) for i in range(4)]

        def four(v, sign):
            (ar, ai), (br, bi), (cr, ci), (dr, di) = v
            pr, pi_, mr, mi = ar + cr, ai + ci, ar - cr, ai - ci
            qr, qi, nr, ni = br + dr, bi + di, br - dr, bi - di
            tr_, ti = -sign * ni, sign * nr
            return [(pr + qr, pi_ + qi), (mr + tr_, mi + ti), (pr - qr, pi_ - qi), (mr - tr_, mi - ti)]

        x = four(g, -1.0)
        prod = []
        for m in range(4):
            hr = psf[0, pl.ds(m * PART0 + start, step), :]
            hi = psf[1, pl.ds(m * PART0 + start, step), :]
            xr, xi = x[m]
            prod.append((xr * hr - xi * hi, xr * hi + xi * hr))
        for i, pair in enumerate(four(prod, 1.0)):
            for part in range(2):
                q_high, q_low = split(pair[part])
                rows = pl.ds(part * PART0 + start, step)
                q_s[0, i, rows, :] = q_high
                q_s[1, i, rows, :] = q_low
        return carry

    lax.fori_loop(0, PART0 // step, middle, 0)

    copies[3].wait()
    copies[4].wait()
    for i in range(4):
        high, low = rback[0, i], rback[1, i]
        z = dot(high, q_s[0, i]) + (dot(high, q_s[1, i]) + dot(low, q_s[0, i]))
        z_high, z_low = split(z)
        sums = []
        for part in range(2):
            rows = slice(part * 128, (part + 1) * 128)
            sums.append(
                dot(z_high[rows], back[2 * part])
                + (dot(z_high[rows], back[2 * part + 1]) + dot(z_low[rows], back[2 * part]))
            )
        for side, value in enumerate((sums[0] - sums[1], sums[0] + sums[1])):
            for level, piece in enumerate(split(value)):
                for j in range(4):
                    s_s[level, j, i * 128 : (i + 1) * 128, side * 128 : (side + 1) * 128] = (
                        piece[:, j * 128 : (j + 1) * 128]
                    )

    def gather(band, carry):
        base = pl.multiple_of(band * 16, 16)
        code = tm[band, 0]
        hot = hot_of(code, 256)
        mask = row16 == jnp.broadcast_to(code[0:1, :] >> 8, (16, 256))
        left = jnp.concatenate(
            [s_s[level, j, pl.ds(i * 128 + base, 16), :] for level in range(2) for j in range(4) for i in range(4)],
            axis=0,
        )
        both = dot(left, hot)
        total = both[:256] + both[256:]
        for c in range(CELLS):
            tg[band, c : c + 1, :] = jnp.sum(
                jnp.where(mask, total[c * 16 : (c + 1) * 16, :], 0.0), axis=0, keepdims=True
            )
        return carry

    lax.fori_loop(0, BANDS, gather, 0)
    halves = []
    for eh in range(2):
        quarter = []
        for bh in range(2):
            group = [tg[bh * 4 + band, :, eh * 128 : (eh + 1) * 128] for band in range(4)]
            quarter.append(jnp.concatenate(chunk_swap(group, lane16), axis=0))
        halves.append(jnp.concatenate(quarter, axis=1))
    out_ref[...] = jnp.transpose(jnp.concatenate(halves, axis=0))


def conv(strip, received, psf):
    fwd, back, rfwd, rback = tables()
    any_spec = pl.BlockSpec(memory_space=pl.ANY)
    return pl.pallas_call(
        conv_kernel,
        out_shape=jax.ShapeDtypeStruct((BANDS * BLOCKS, 128), F32),
        in_specs=[
            pl.BlockSpec(memory_space=pltpu.SMEM),
            pl.BlockSpec(memory_space=pltpu.VMEM),
            any_spec, any_spec, any_spec, any_spec, any_spec,
        ],
        out_specs=pl.BlockSpec(memory_space=pltpu.VMEM),
        scratch_shapes=[
            pltpu.VMEM((4, 1024, STRIP), BF),
            pltpu.VMEM((2, 4, 2 * PART0, 256), BF),
            pltpu.VMEM((2, L0, STRIP), F32),
            pltpu.VMEM((2, 4, 256, 2 * PART0), BF),
            pltpu.VMEM((4, STRIP, 512), BF),
            pltpu.VMEM((BANDS, 3, CELLS, 256), F32),
            pltpu.VMEM((BANDS, 3, 8, 256), jnp.int32),
            pltpu.VMEM((2, ROWS, 1024), BF),
            pltpu.VMEM((2, ROWS, 1024), BF),
            pltpu.VMEM((2, 4, 256, STRIP), BF),
            pltpu.VMEM((2, 4, 2 * PART0, STRIP), BF),
            pltpu.VMEM((2, 4, ROWS, 256), BF),
            pltpu.VMEM((BANDS, CELLS, 256), F32),
            pltpu.SemaphoreType.DMA((5,)),
        ],
        compiler_params=pltpu.CompilerParams(vmem_limit_bytes=VMEM_LIMIT),
        name="conv",
    )(strip, received, jnp.asarray(fwd), jnp.asarray(rfwd), psf, jnp.asarray(rback), jnp.asarray(back))


def spread_kernel(meta_ref, back_ref, base_ref, out_ref):
    rows = base_ref.shape[0]
    summed = back_ref[0:BLOCKS, :]
    for f in range(1, BANDS):
        summed = summed + back_ref[f * BLOCKS : (f + 1) * BLOCKS, :]
    meta = meta_ref[...]
    target, rank, right = meta[:, 0:1], meta[:, 1:2], meta[:, 2:3]
    hot = jnp.where(iota((rows, BLOCKS), 1) == target, 1.0, 0.0).astype(BF)
    picked = jnp.zeros((rows, 128), F32)
    for piece in split3(summed):
        picked = picked + dot(hot, piece)
    lane = iota((rows, 128), 1)
    picked = jnp.where((lane >> 4) == rank, picked, 0.0)
    plain = jnp.where(right == 1, picked, 0.0)
    sides = jnp.concatenate([plain, picked - plain], axis=1)
    krow, nlane = iota((256, 512), 0), iota((256, 512), 1)
    have_j = (krow >> 2) & 3
    have_j = jnp.where(krow >= 128, 3 - have_j, have_j)
    match = (have_j == ((nlane >> 4) & 3)) & ((krow & 3) == (nlane >> 7))
    weights = jnp.where(match, 1.0, 0.0).astype(BF)
    up = jnp.zeros((rows, 512), F32)
    for piece in split3(sides):
        up = up + dot(piece, weights)
    for i in range(4):
        value = up[:, i * 128 : (i + 1) * 128]
        for m in range(8):
            spot = slice(i * 1024 + m * 128, i * 1024 + (m + 1) * 128)
            out_ref[:, spot] = (base_ref[:, spot].astype(F32) + value).astype(BF)


def spread(meta, returned, base_grad):
    step = 64
    return pl.pallas_call(
        spread_kernel,
        grid=(SLOTS // step,),
        out_shape=jax.ShapeDtypeStruct((SLOTS, 4096), BF),
        in_specs=[
            pl.BlockSpec((step, 128), lambda g: (g, 0)),
            pl.BlockSpec((BANDS * BLOCKS, 128), lambda g: (0, 0)),
            pl.BlockSpec((step, 4096), lambda g: (g, 0)),
        ],
        out_specs=pl.BlockSpec((step, 4096), lambda g: (g, 0)),
        compiler_params=pltpu.CompilerParams(vmem_limit_bytes=VMEM_LIMIT),
        name="spread",
    )(meta, returned, base_grad)


def exchange(x):
    return lax.all_to_all(x, ("fft", "tiles"), split_axis=0, concat_axis=0, tiled=True)


def local(cotangent, base_grad, tile_place, tile_count, psf_spectrum):
    strip = lax.axis_index("fft").astype(jnp.int32).reshape(1, 1)
    message, meta = pool(cotangent, tile_place, tile_count)
    received = exchange(message)
    partial = conv(strip, received, psf_spectrum)
    returned = exchange(partial)
    return spread(meta, returned, base_grad)


def solution(mesh):
    return jax.shard_map(
        local,
        mesh=mesh,
        in_specs=(
            P(("tiles", "fft"), None),
            P(("tiles", "fft"), None),
            P(("tiles", "fft")),
            P(("tiles", "fft")),
            P(None, None, "fft"),
        ),
        out_specs=P(("tiles", "fft"), None),
        check_vma=False,
    )
```

time: 949 us -> 82.7 us (0.09)
  waiting for transfers between devices: 471 us -> 20 us
  matrix products: 344 us -> 0 us
  local copies, waits for them, and re-layouts: 68.1 us -> 2.04 us
  Pallas kernels: 0 us -> 25.3 us
  starting transfers between devices: 34.8 us -> 15.7 us
  blocking collectives: 0 us -> 18.8 us
  between operations: 14.9 us -> 0.69 us
  other arithmetic: 9.66 us -> 0 us
    all_gather x1 -> x0, waiting for transfers between devices: 426 us -> none  [local(): piece = lax.all_gather(sens_patch, 'tiles', axis=0, tiled=True)]
    dot_general x12 -> x0, matrix products: 344 us -> none  [product(): jnp.dot(left, right, precision=lax.Precision.HIGHEST, preferred_element_t...]
    pallas_call x0 -> x3, Pallas kernels: none -> 25.3 us  [the longest x1 17.8 us: conv(): pl.pallas_call(conv_kernel, out_shape=jax.ShapeDtypeStruct((BANDS * BLOCK...]
    all_to_all x4 -> x1, waiting for transfers between devices: 41.5 us -> 20 us  [exchange(): lax.all_to_all(x, ('fft', 'tiles'), split_axis=0, concat_axis=0, tiled=True)]
    reshape x6 -> x0, local copies, waits for them, and re-layouts: 20.4 us -> none  [the longest x1 10 us: local(): sensitivity.reshape(tile_rows, TCELL, tile_cols, TCELL)]
    all_to_all x0 -> x1, blocking collectives: none -> 18.8 us  [exchange(): lax.all_to_all(x, ('fft', 'tiles'), split_axis=0, concat_axis=0, tiled=True)]
    all_to_all x4 -> x1, starting transfers between devices: 31.1 us -> 15.7 us  [exchange(): lax.all_to_all(x, ('fft', 'tiles'), split_axis=0, concat_axis=0, tiled=True)]
    unnamed x14 -> x3, local copies, waits for them, and re-layouts: 12.5 us -> 0.71 us
  transfers between devices with their start and end apart: 7 -> 1, of which waited for: 7 -> 1; matrix products, arithmetic and copies ran while one was open for 1% -> 0% of each run, Pallas kernels for 0% -> 0%
where the time goes in v1:
time: 82.7 us; the launch traced here: 82.5 us
  Pallas kernels  25.3 us (31%)
  waiting for transfers between devices  20 us (24%)
  blocking collectives  18.8 us (23%)
  starting transfers between devices  15.7 us (19%)
  local copies, waits for them, and re-layouts  2.04 us (2%)
    all_to_all x1, waiting for transfers between devices, exchange(): lax.all_to_all(x, ('fft', 'tiles'), split_axis=0, concat_axis=0, tiled=True)  20 us
    all_to_all x1, blocking collectives, exchange(): lax.all_to_all(x, ('fft', 'tiles'), split_axis=0, concat_axis=0, tiled=True)  18.8 us
    pallas_call x1, Pallas kernels, conv(): pl.pallas_call(conv_kernel, out_shape=jax.ShapeDtypeStruct((BANDS * BLOCK...  17.8 us
    all_to_all x1, starting transfers between devices, exchange(): lax.all_to_all(x, ('fft', 'tiles'), split_axis=0, concat_axis=0, tiled=True)  15.7 us
    pallas_call x1, Pallas kernels, spread(): pl.pallas_call(spread_kernel, grid=(SLOTS // step,), out_shape=jax.ShapeD...  4.77 us
    pallas_call x1, Pallas kernels, pool(): pl.pallas_call(pool_kernel, out_shape=(jax.ShapeDtypeStruct((BANDS * BLOC...  2.69 us
  transfers between devices with their start and end apart: 1, of which 1 were waited for; matrix products, arithmetic and copies ran while one was open for 0% of the time, Pallas kernels for 0%

profile of v1, /device:TPU:1, one launch (start us, length us, event | category | flops | bytes accessed | tf_op | source)
XLA Modules:
  0.0 82.5 jit_solution(16619397351000217040)
XLA Ops:
  0.7 0.0 copy-start
  0.7 0.7 copy-done
  1.3 2.7 %pool.1 = (f32[256,512]{1,0:T(8,128)S(1)}, s32[256,128]{1,0:T(8,128)S(1)}) custom-call(s32[1]{0:T(128)S(6)} %copy.15.count_ref, s32[1,256]{1,0:T(1,128)S(1)} %bitcast.14, bf16[256,4096]{1,0:T(8,128)(2,1)} %cot_hbm.1), custom_call_target="tpu_custom_call" | custom-call | tf_op jit(solution)/shard_map/pool/pallas_call | solution.py:174
  4.0 1.3 %copy.10 = f32[256,1,512]{2,1,0:T(1,128)} copy(f32[256,1,512]{2,0,1:T(8,128)S(1)} %bitcast.13) | data formatting | bytes 1048576 | tf_op jit(solution)/shard_map/all_to_all | solution.py:461
  5.4 15.7 %all-to-all-start = ((f32[256,1,512]{2,1,0:T(1,128)}), f32[256,1,512]{2,1,0:T(1,128)S(1)}, u32[]{:S(2)}, u32[]{:S(2)}) async-start(f32[256,1,512]{2,1,0:T(1,128)} %copy.10), calls=%async_computation | async-start | bytes 1048576 | tf_op jit(solution)/shard_map/all_to_all | solution.py:461
  21.0 20.0 %all-to-all-done = f32[256,1,512]{2,1,0:T(1,128)S(1)} async-done(((f32[256,1,512]{2,1,0:T(1,128)}), f32[256,1,512]{2,1,0:T(1,128)S(1)}, u32[]{:S(2)}, u32[]{:S(2)}) %all-to-all-start) | async-done | bytes 524320 | tf_op jit(solution)/shard_map/all_to_all | solution.py:461
  41.1 17.8 %conv.1 = f32[256,128]{1,0:T(8,128)S(1)} custom-call(s32[1,1]{1,0:T(1,128)} %bitcast.1.f_ref, f32[256,512]{1,0:T(8,128)S(1)} %bitcast.10, bf16[8,4,1024,256]{3,2,1,0:T(8,128)(2,1)} %constant.12.clone.fwd_hbm, bf16[2,4,768,256]{3,2,1,0:T(8,128)(2,1)} %constant.13.clone.rfwd_hbm, f32[2,1536,256]{2,1,0:T(8,128)} %psf_hbm.1, ...), custom_call_target="tpu_custom_call" | custom-call | tf_op jit(solution)/shard_map/conv/pallas_call | solution.py:383
  58.9 18.8 %all_to_all.22 = f32[256,1,128]{2,1,0:T(1,128)S(1)} all-to-all(f32[256,1,128]{2,1,0:T(1,128)S(1)} %bitcast.11), channel_id=1, replica_groups=mesh['tiles'=32,'fft'=8] {'fft','tiles'}, dimensions={0} | all-to-all | bytes 262144 | tf_op jit(solution)/shard_map/all_to_all | solution.py:461
  77.7 4.8 %spread.1 = bf16[256,4096]{1,0:T(8,128)(2,1)} custom-call(s32[256,128]{1,0:T(8,128)S(1)} %get-tuple-element.7.meta_ref, f32[256,128]{1,0:T(8,128)S(1)} %bitcast.12, bf16[256,4096]{1,0:T(8,128)(2,1)} %base_ref.1), custom_call_target="tpu_custom_call" | custom-call | tf_op jit(solution)/shard_map/spread/pallas_call | solution.py:445
  (1 shorter events, 0.0 us)
Async XLA Ops:
  0.7 0.7 copy-start
  5.4 35.7 %all-to-all-start = ((f32[256,1,512]{2,1,0:T(1,128)}), f32[256,1,512]{2,1,0:T(1,128)S(1)}, u32[]{:S(2)}, u32[]{:S(2)}) async-start(f32[256,1,512]{2,1,0:T(1,128)} %copy.10), calls=%async_computation | async-start | bytes 1048576 | tf_op jit(solution)/shard_map/all_to_all | solution.py:461

commit v2 on v1

v2 whole, which is shorter than its diff:
```python
import functools
import math

import jax
import jax.numpy as jnp
import ml_dtypes
import numpy as np
from jax import lax
from jax.experimental import pallas as pl
from jax.experimental.pallas import tpu as pltpu
from jax.sharding import PartitionSpec as P

BANDS = 8
BLOCKS = 32
BUCKET = 8
SLOTS = 256
SUB = 16
TCELL = 4
CELLS = 16
TILE_ROWS = 16
TILE_COLS = 256
ROWS = 512
L0 = 1536
L1 = 2048
STRIP = 256
HALF = 128
PART0 = L0 // 4
STEP = 128
CHUNKS = PART0 // STEP
PAIRS = BANDS // 2
BF = jnp.bfloat16
F32 = jnp.float32
UNROLL = 4
VMEM_LIMIT = 52 * 1024 * 1024


def split_np(table):
    high = table.astype(ml_dtypes.bfloat16)
    low = (table - high.astype(np.float64)).astype(ml_dtypes.bfloat16)
    return high, low


@functools.lru_cache(maxsize=None)
def tables():
    k = np.arange(L1)
    u = np.arange(L1 // 2).reshape(256, 4).T.reshape(-1)
    angle = (np.outer(2 * u + 1, k) % (2 * L1)) * (math.pi / L1)
    cos, sin = np.cos(angle), np.sin(angle)

    def strips(table):
        return table.reshape(table.shape[0], BANDS, STRIP).transpose(1, 0, 2)

    ch, cl = split_np(strips(cos))
    sh, sl = split_np(strips(-sin))
    fwd = np.stack([ch, cl, sh, sl], axis=1)
    near = (u < 2 * STRIP)
    scale = 1.0 / (L0 * L1)
    ch, cl = split_np(strips(cos[near]).transpose(0, 2, 1) * scale)
    sh, sl = split_np(strips(sin[near]).transpose(0, 2, 1) * scale)
    back = np.stack([ch, cl, sh, sl], axis=1)
    k0 = np.arange(PART0)
    rows = []
    for i in range(4):
        angle = (np.outer(k0, 4 * np.arange(128) + i) % L0) * (2 * math.pi / L0)
        c, s = np.cos(angle), np.sin(angle)
        rows.append(np.block([[c, s], [-s, c]]))
    rows = np.stack(rows)
    both = np.stack(split_np(rows)).reshape(2, 4, 2, CHUNKS, STEP, 256)
    rfwd = both.transpose(1, 3, 0, 2, 4, 5).reshape(4, CHUNKS, 4 * STEP, 256)
    rback = np.concatenate(split_np(rows.transpose(0, 2, 1)), axis=1)
    return fwd, back, rfwd, rback


def split(x):
    high = x.astype(BF)
    low = (x - high.astype(F32)).astype(BF)
    return high, low


def split3(x):
    high = x.astype(BF)
    rest = x - high.astype(F32)
    mid = rest.astype(BF)
    low = (rest - mid.astype(F32)).astype(BF)
    return high, mid, low


def dot(a, b):
    return jnp.dot(a, b, preferred_element_type=F32)


def dot_nt(a, b):
    return lax.dot_general(a, b, (((1,), (1,)), ((), ())), preferred_element_type=F32)


def iota(shape, dim):
    return lax.broadcasted_iota(jnp.int32, shape, dim)


def pool_kernel(count_ref, place_hbm, cot_hbm, msg_ref, meta_ref, place_ref, cot, sems):
    fetch = pltpu.make_async_copy(place_hbm, place_ref, sems.at[4])
    fetch.start()
    copies = [
        pltpu.make_async_copy(
            cot_hbm.at[:, pl.ds(i * 1024, 1024)], cot.at[:, pl.ds(i * 1024, 1024)], sems.at[i]
        )
        for i in range(4)
    ]
    for copy in copies:
        copy.start()
    count = count_ref[0]
    fetch.wait()
    place_row = place_ref[...]
    square = (SLOTS, SLOTS)
    down, across = iota(square, 0), iota(square, 1)

    def fields(place, live):
        column = place & (BLOCKS * TILE_COLS - 1)
        row = (place >> 13) & (TILE_ROWS - 1)
        target = jnp.where(live, column >> 8, -8)
        return row, target, column & (TILE_COLS - 1)

    live_row = iota((1, SLOTS), 1) < count
    _, target_row, tc_row = fields(place_row, live_row)
    place_col = jnp.sum(
        jnp.where(down == across, place_row.astype(F32), 0.0), axis=1, keepdims=True
    ).astype(jnp.int32)
    live_col = iota((SLOTS, 1), 0) < count
    tr_col, target_col, tc_col = fields(place_col, live_col)
    before = (target_row == target_col) & (across < down) & live_row
    rank_col = jnp.sum(jnp.where(before, 1.0, 0.0), axis=1, keepdims=True).astype(jnp.int32)
    right_col = tc_col >= HALF
    lane = iota((SLOTS, 128), 1)
    meta_ref[...] = jnp.where(
        lane == 0, target_col, jnp.where(lane == 1, rank_col, right_col.astype(jnp.int32))
    )
    b = iota((BLOCKS, SLOTS), 0)
    right_row = tc_row >= HALF
    hot_own = target_row == b
    hot_left = (target_row == b - 1) & right_row & live_row
    hot_right = (target_row == b + 1) & (~right_row) & live_row
    hot = jnp.concatenate(
        [jnp.where(h, 1.0, 0.0) for h in (hot_own, hot_left, hot_right)], axis=0
    ).astype(BF)
    code_own = 1 + tr_col * 256 + jnp.where(right_col, tc_col - HALF, 255 - tc_col)
    code_halo = 1 + tr_col * 256 + jnp.where(right_col, 255 - tc_col, tc_col)
    mark_own = jnp.where(lane == rank_col, code_own, 0).astype(F32)
    mark_halo = jnp.where((lane & 7) == rank_col, code_halo, 0).astype(F32)
    prow, plane = iota((256, 256), 0), iota((256, 256), 1)
    want_j = (plane >> 2) & 3
    want_j = jnp.where(plane >= 128, 3 - want_j, want_j)
    match_j = ((prow >> 4) & 3) == want_j
    total = jnp.zeros((SLOTS, 256), F32)
    for i in range(4):
        weights = jnp.where(match_j & ((plane & 3) == i), 1.0, 0.0).astype(BF)
        copies[i].wait()
        for c in range(4):
            total = total + dot(cot[:, i * 1024 + c * 256 : i * 1024 + (c + 1) * 256], weights)
    plain, flipped = total[:, :128], total[:, 128:]
    here = (lane >> 4) == rank_col
    own = jnp.where(here, jnp.where(right_col, plain, flipped), 0.0)
    halo = jnp.where(here, jnp.where(right_col, flipped, plain), 0.0)
    loads = jnp.concatenate([own, halo, mark_own, mark_halo], axis=1)
    out = jnp.zeros((3 * BLOCKS, 512), F32)
    for piece in split3(loads):
        out = out + dot(hot, piece)
    lane32 = iota((BLOCKS, 128), 1)
    marks = jnp.where(
        lane32 < 8,
        out[0:32, 256:384],
        jnp.where(lane32 < 16, out[32:64, 384:512], jnp.where(lane32 < 24, out[64:96, 384:512], 0.0)),
    )
    message = [out[0:32, 0:128], out[32:64, 128:256], out[64:96, 128:256], marks]
    for f in range(PAIRS):
        for a in range(4):
            msg_ref[pl.ds(f * BLOCKS * 4 + a, BLOCKS, stride=4), :] = message[a]


def pool(cotangent, tile_place, tile_count):
    return pl.pallas_call(
        pool_kernel,
        out_shape=(
            jax.ShapeDtypeStruct((PAIRS * BLOCKS * 4, 128), F32),
            jax.ShapeDtypeStruct((SLOTS, 128), jnp.int32),
        ),
        in_specs=[
            pl.BlockSpec(memory_space=pltpu.SMEM),
            pl.BlockSpec(memory_space=pl.ANY),
            pl.BlockSpec(memory_space=pl.ANY),
        ],
        out_specs=(
            pl.BlockSpec(memory_space=pltpu.VMEM),
            pl.BlockSpec(memory_space=pltpu.VMEM),
        ),
        scratch_shapes=[
            pltpu.VMEM((1, SLOTS), jnp.int32),
            pltpu.VMEM((SLOTS, 4096), BF),
            pltpu.SemaphoreType.DMA((5,)),
        ],
        compiler_params=pltpu.CompilerParams(vmem_limit_bytes=VMEM_LIMIT),
        name="pool",
    )(tile_count, tile_place.reshape(1, SLOTS), cotangent)


def chunk_swap(pieces, lane):
    out = []
    for band in range(4):
        value = None
        for e in range(4):
            moved = pieces[e] if e == band else pltpu.roll(pieces[e], ((e - band) * 32) % 128, 1)
            value = moved if value is None else jnp.where((lane >> 5) == e, moved, value)
        out.append(value)
    return out


def conv_kernel(
    f_ref, near_ref, pair_ref, fwd_hbm, rfwd_hbm, psf_hbm, rback_hbm, back_hbm, out_ref,
    fwd, rfwd, psf, rback, back, tv, tm, e_s, o_s, y_s, g_s, q_s, z_s, s_s, tg, sems,
):
    f = f_ref[0, 0]
    copies = [
        pltpu.make_async_copy(fwd_hbm.at[f], fwd, sems.at[0]),
        pltpu.make_async_copy(rfwd_hbm, rfwd, sems.at[1]),
        pltpu.make_async_copy(psf_hbm, psf, sems.at[2]),
        pltpu.make_async_copy(rback_hbm, rback, sems.at[3]),
        pltpu.make_async_copy(back_hbm.at[f], back, sems.at[4]),
    ]
    for copy in copies:
        copy.start()
    core = f & 1

    lane16 = iota((16, 128), 1)
    lane8 = iota((8, 128), 1)
    for half, ref in enumerate((near_ref, pair_ref)):
        turned = [jnp.transpose(ref[pl.ds(a, 128, stride=4), :]) for a in range(4)]
        for nbr in range(3):
            for eh in range(2):
                group = [turned[nbr][(eh * 4 + e) * 16 : (eh * 4 + e + 1) * 16, :] for e in range(4)]
                for x, value in enumerate(chunk_swap(group, lane16)):
                    tv[half * PAIRS + x, nbr, :, eh * 128 : (eh + 1) * 128] = value
                marks = turned[3][nbr * 8 : nbr * 8 + 8, :]
                group = [
                    jnp.broadcast_to(marks[eh * 4 + e : eh * 4 + e + 1, :], (8, 128)) for e in range(4)
                ]
                for x, value in enumerate(chunk_swap(group, lane8)):
                    tm[half * PAIRS + x, nbr, :, eh * 128 : (eh + 1) * 128] = value.astype(jnp.int32) - 1

    row16 = iota((16, 256), 0)

    def band_of(spot):
        return 2 * (spot & (PAIRS - 1)) + (core ^ (spot >> 2))

    def hot_of(code, rows):
        place = jnp.broadcast_to(code[0:1, :] & 255, (rows, 256))
        return jnp.where(iota((rows, 256), 0) == place, 1.0, 0.0).astype(BF)

    def scatter(spot, carry):
        base = pl.multiple_of(band_of(spot) * 16, 16)
        outs = []
        for nbr in range(3):
            code = tm[spot, nbr]
            mask = row16 == jnp.broadcast_to(code[0:1, :] >> 8, (16, 256))
            values = tv[spot, nbr]
            high = values.astype(BF).astype(F32)
            low = values - high
            parts = []
            for piece in (high, low):
                for c in range(CELLS):
                    parts.append(
                        jnp.where(mask, jnp.broadcast_to(piece[c : c + 1, :], (16, 256)), 0.0).astype(BF)
                    )
            left = jnp.concatenate(parts, axis=0)
            both = dot_nt(left, hot_of(code, 256 if nbr == 0 else 128))
            outs.append(both[:256] + both[256:])
        near_r, near_l = outs[0][:, :128], outs[0][:, 128:]
        far_l, far_r = outs[1], outs[2]
        for ref, near, far in ((e_s, near_r + near_l, far_r + far_l), (o_s, near_r - near_l, far_r - far_l)):
            for part, value in enumerate((near, far)):
                for level, piece in enumerate(split(value)):
                    for j in range(4):
                        for i in range(4):
                            ref[pl.ds(level * ROWS + i * 128 + base, 16),
                                j * 256 + part * 128 : j * 256 + (part + 1) * 128] = (
                                piece[(j * 4 + i) * 16 : (j * 4 + i + 1) * 16, :]
                            )
        return carry

    lax.fori_loop(0, BANDS, scatter, 0, unroll=UNROLL)

    copies[0].wait()
    for part, ref in enumerate((e_s, o_s)):
        first = dot(ref[...], fwd[2 * part])
        second = dot(ref[:ROWS, :], fwd[2 * part + 1])
        y = first[:ROWS] + (first[ROWS:] + second)
        for level, piece in enumerate(split(y)):
            for i in range(4):
                y_s[level, i, part * 128 : (part + 1) * 128, :] = piece[i * 128 : (i + 1) * 128]

    copies[1].wait()
    copies[2].wait()

    def four(v, sign):
        (ar, ai), (br, bi), (cr, ci), (dr, di) = v
        pr, pi_, mr, mi = ar + cr, ai + ci, ar - cr, ai - ci
        qr, qi, nr, ni = br + dr, bi + di, br - dr, bi - di
        if sign > 0:
            return [(pr + qr, pi_ + qi), (mr - ni, mi + nr), (pr - qr, pi_ - qi), (mr + ni, mi - nr)]
        return [(pr + qr, pi_ + qi), (mr + ni, mi - nr), (pr - qr, pi_ - qi), (mr - ni, mi + nr)]

    for chunk in range(CHUNKS):
        for i in range(4):
            first = dot(rfwd[i, chunk], y_s[0, i])
            second = dot(rfwd[i, chunk, : 2 * STEP, :], y_s[1, i])
            g_s[chunk, i] = first[: 2 * STEP] + (first[2 * STEP :] + second)
        for r in range(0, STEP, 16):
            for lanes in (slice(0, 128), slice(128, 256)):
                g = [(g_s[chunk, i, r : r + 16, lanes], g_s[chunk, i, STEP + r : STEP + r + 16, lanes])
                     for i in range(4)]
                prod = []
                for m, (xr, xi) in enumerate(four(g, -1)):
                    rows = slice(m * PART0 + chunk * STEP + r, m * PART0 + chunk * STEP + r + 16)
                    hr, hi = psf[0, rows, lanes], psf[1, rows, lanes]
                    prod.append((xr * hr - xi * hi, xr * hi + xi * hr))
                for i, pair in enumerate(four(prod, 1)):
                    for part in range(2):
                        rows = slice(part * PART0 + chunk * STEP + r, part * PART0 + chunk * STEP + r + 16)
                        for level, piece in enumerate(split(pair[part])):
                            q_s[level, i, rows, lanes] = piece

    copies[3].wait()
    for i in range(4):
        first = dot(rback[i], q_s[0, i])
        second = dot(rback[i, :256, :], q_s[1, i])
        z = first[:256] + (first[256:] + second)
        for level, piece in enumerate(split(z)):
            for part in range(2):
                z_s[part, level * ROWS + i * 128 : level * ROWS + (i + 1) * 128, :] = (
                    piece[part * 128 : (part + 1) * 128]
                )
    copies[4].wait()
    for j in range(4):
        lanes = slice(j * 128, (j + 1) * 128)
        sums = []
        for part in range(2):
            first = dot(z_s[part], back[2 * part, :, lanes])
            second = dot(z_s[part, :ROWS, :], back[2 * part + 1, :, lanes])
            sums.append(first[:ROWS] + (first[ROWS:] + second))
        for side, value in enumerate((sums[0] - sums[1], sums[0] + sums[1])):
            for level, piece in enumerate(split(value)):
                s_s[level, j, :, side * 128 : (side + 1) * 128] = piece

    def gather(spot, carry):
        base = pl.multiple_of(band_of(spot) * 16, 16)
        code = tm[spot, 0]
        hot = hot_of(code, 256)
        mask = row16 == jnp.broadcast_to(code[0:1, :] >> 8, (16, 256))
        left = jnp.concatenate(
            [s_s[level, j, pl.ds(i * 128 + base, 16), :] for level in range(2) for j in range(4) for i in range(4)],
            axis=0,
        )
        both = dot(left, hot)
        total = both[:256] + both[256:]
        for c in range(CELLS):
            tg[spot, c : c + 1, :] = jnp.sum(
                jnp.where(mask, total[c * 16 : (c + 1) * 16, :], 0.0), axis=0, keepdims=True
            )
        return carry

    lax.fori_loop(0, BANDS, gather, 0, unroll=UNROLL)
    for half in range(2):
        pieces = []
        for eh in range(2):
            group = [tg[half * PAIRS + x, :, eh * 128 : (eh + 1) * 128] for x in range(4)]
            pieces += chunk_swap(group, lane16)
        turned = jnp.transpose(jnp.concatenate(pieces, axis=0))
        for x in range(PAIRS):
            base = pl.multiple_of(band_of(half * PAIRS + x) * BLOCKS, BLOCKS)
            out_ref[pl.ds(base, BLOCKS), :] = turned[x * BLOCKS : (x + 1) * BLOCKS, :]


def conv(strip, near, pair, psf):
    fwd, back, rfwd, rback = tables()
    any_spec = pl.BlockSpec(memory_space=pl.ANY)
    vmem_spec = pl.BlockSpec(memory_space=pltpu.VMEM)
    return pl.pallas_call(
        conv_kernel,
        out_shape=jax.ShapeDtypeStruct((BANDS * BLOCKS, 128), F32),
        in_specs=[
            pl.BlockSpec(memory_space=pltpu.SMEM), vmem_spec, vmem_spec,
            any_spec, any_spec, any_spec, any_spec, any_spec,
        ],
        out_specs=vmem_spec,
        scratch_shapes=[
            pltpu.VMEM((4, 1024, STRIP), BF),
            pltpu.VMEM((4, CHUNKS, 4 * STEP, 256), BF),
            pltpu.VMEM((2, L0, STRIP), F32),
            pltpu.VMEM((4, 512, 2 * PART0), BF),
            pltpu.VMEM((4, STRIP, 512), BF),
            pltpu.VMEM((BANDS, 3, CELLS, 256), F32),
            pltpu.VMEM((BANDS, 3, 8, 256), jnp.int32),
            pltpu.VMEM((2 * ROWS, 1024), BF),
            pltpu.VMEM((2 * ROWS, 1024), BF),
            pltpu.VMEM((2, 4, 256, STRIP), BF),
            pltpu.VMEM((CHUNKS, 4, 2 * STEP, STRIP), F32),
            pltpu.VMEM((2, 4, 2 * PART0, STRIP), BF),
            pltpu.VMEM((2, 2 * ROWS, STRIP), BF),
            pltpu.VMEM((2, 4, ROWS, 256), BF),
            pltpu.VMEM((BANDS, CELLS, 256), F32),
            pltpu.SemaphoreType.DMA((5,)),
        ],
        compiler_params=pltpu.CompilerParams(vmem_limit_bytes=VMEM_LIMIT),
        name="conv",
    )(strip, near, pair, jnp.asarray(fwd), jnp.asarray(rfwd), psf, jnp.asarray(rback), jnp.asarray(back))


def spread_kernel(meta_ref, back_ref, base_hbm, out_hbm, base, done, sems):
    loads, stores = [], []
    for i in range(4):
        lanes = pl.ds(i * 1024, 1024)
        loads.append(pltpu.make_async_copy(base_hbm.at[:, lanes], base.at[:, lanes], sems.at[i]))
        stores.append(pltpu.make_async_copy(done.at[:, lanes], out_hbm.at[:, lanes], sems.at[4 + i]))
    for load in loads:
        load.start()
    summed = back_ref[0:BLOCKS, :]
    for f in range(1, BANDS):
        summed = summed + back_ref[f * BLOCKS : (f + 1) * BLOCKS, :]
    meta = meta_ref[...]
    target, rank, right = meta[:, 0:1], meta[:, 1:2], meta[:, 2:3]
    hot = jnp.where(iota((SLOTS, BLOCKS), 1) == target, 1.0, 0.0).astype(BF)
    picked = jnp.zeros((SLOTS, 128), F32)
    for piece in split3(summed):
        picked = picked + dot(hot, piece)
    lane = iota((SLOTS, 128), 1)
    picked = jnp.where((lane >> 4) == rank, picked, 0.0)
    plain = jnp.where(right == 1, picked, 0.0)
    sides = split3(jnp.concatenate([plain, picked - plain], axis=1))
    krow, nlane = iota((256, 128), 0), iota((256, 128), 1)
    have_j = (krow >> 2) & 3
    have_j = jnp.where(krow >= 128, 3 - have_j, have_j)
    match = have_j == ((nlane >> 4) & 3)
    for i in range(4):
        weights = jnp.where(match & ((krow & 3) == i), 1.0, 0.0).astype(BF)
        value = dot(sides[0], weights) + (dot(sides[1], weights) + dot(sides[2], weights))
        loads[i].wait()
        for m in range(8):
            spot = slice(i * 1024 + m * 128, i * 1024 + (m + 1) * 128)
            done[:, spot] = (base[:, spot].astype(F32) + value).astype(BF)
        stores[i].start()
    for store in stores:
        store.wait()


def spread(meta, returned, base_grad):
    return pl.pallas_call(
        spread_kernel,
        out_shape=jax.ShapeDtypeStruct((SLOTS, 4096), BF),
        in_specs=[
            pl.BlockSpec(memory_space=pltpu.VMEM),
            pl.BlockSpec(memory_space=pltpu.VMEM),
            pl.BlockSpec(memory_space=pl.ANY),
        ],
        out_specs=pl.BlockSpec(memory_space=pl.ANY),
        scratch_shapes=[
            pltpu.VMEM((SLOTS, 4096), BF),
            pltpu.VMEM((SLOTS, 4096), BF),
            pltpu.SemaphoreType.DMA((8,)),
        ],
        compiler_params=pltpu.CompilerParams(vmem_limit_bytes=16 * 1024 * 1024),
        name="spread",
    )(meta, returned, base_grad)


def exchange(x, groups=None):
    return lax.all_to_all(
        x, ("fft", "tiles"), split_axis=0, concat_axis=0, axis_index_groups=groups, tiled=True
    )


def local(cotangent, base_grad, tile_place, tile_count, psf_spectrum):
    strip = lax.axis_index("fft").astype(jnp.int32).reshape(1, 1)
    message, meta = pool(cotangent, tile_place, tile_count)
    groups = [[f * BLOCKS + t for f in range(c, BANDS, 2) for t in range(BLOCKS)] for c in range(2)]
    near = exchange(message.reshape(PAIRS * BLOCKS, 4, 128), groups).reshape(-1, 128)
    pair = lax.ppermute(near, "fft", [(f, f ^ 1) for f in range(BANDS)])
    partial = conv(strip, near, pair, psf_spectrum)
    returned = exchange(partial)
    return spread(meta, returned, base_grad)


def solution(mesh):
    return jax.shard_map(
        local,
        mesh=mesh,
        in_specs=(
            P(("tiles", "fft"), None),
            P(("tiles", "fft"), None),
            P(("tiles", "fft")),
            P(("tiles", "fft")),
            P(None, None, "fft"),
        ),
        out_specs=P(("tiles", "fft"), None),
        check_vma=False,
    )
```

time: 82.7 us -> 70.1 us (0.85)
  blocking collectives: 18.8 us -> 46.7 us
  waiting for transfers between devices: 20 us -> 1.16 us
  starting transfers between devices: 15.7 us -> 2.94 us
  Pallas kernels: 25.3 us -> 17.6 us
  local copies, waits for them, and re-layouts: 2.04 us -> 0.68 us
    all_to_all x1 -> x2, blocking collectives: 18.8 us -> 46.7 us  [exchange(): lax.all_to_all(x, ('fft', 'tiles'), split_axis=0, concat_axis=0, axis_ind...]
    all_to_all x1 -> x0, waiting for transfers between devices: 20 us -> none  [exchange(): lax.all_to_all(x, ('fft', 'tiles'), split_axis=0, concat_axis=0, tiled=True)]
    all_to_all x1 -> x0, starting transfers between devices: 15.7 us -> none  [exchange(): lax.all_to_all(x, ('fft', 'tiles'), split_axis=0, concat_axis=0, tiled=True)]
    pallas_call x1, Pallas kernels: 17.8 us -> 11.8 us  [conv(): pl.pallas_call(conv_kernel, out_shape=jax.ShapeDtypeStruct((BANDS * BLOCK...]
    ppermute x0 -> x1, starting transfers between devices: none -> 2.94 us  [local(): pair = lax.ppermute(near, 'fft', [(f, f ^ 1) for f in range(BANDS)])]
    pallas_call x2, Pallas kernels: 7.46 us -> 5.85 us  [the longest x1 3.16 us: spread(): pl.pallas_call(spread_kernel, out_shape=jax.ShapeDtypeStruct((SLOTS, 4096...]
    all_to_all x1 -> x0, local copies, waits for them, and re-layouts: 1.33 us -> none  [exchange(): lax.all_to_all(x, ('fft', 'tiles'), split_axis=0, concat_axis=0, tiled=True)]
    ppermute x0 -> x1, waiting for transfers between devices: none -> 1.16 us  [local(): pair = lax.ppermute(near, 'fft', [(f, f ^ 1) for f in range(BANDS)])]
where the time goes in v2:
time: 70.1 us; the launch traced here: 69.9 us
  blocking collectives  46.7 us (67%)
  Pallas kernels  17.6 us (25%)
  starting transfers between devices  2.94 us (4%)
  waiting for transfers between devices  1.16 us (2%)
  between operations  0.84 us (1%)
    all_to_all x2, blocking collectives, exchange(): lax.all_to_all(x, ('fft', 'tiles'), split_axis=0, concat_axis=0, axis_ind...  46.7 us
    pallas_call x1, Pallas kernels, conv(): pl.pallas_call(conv_kernel, out_shape=jax.ShapeDtypeStruct((BANDS * BLOCK...  11.8 us
    pallas_call x1, Pallas kernels, spread(): pl.pallas_call(spread_kernel, out_shape=jax.ShapeDtypeStruct((SLOTS, 4096...  3.16 us
    ppermute x1, starting transfers between devices, local(): pair = lax.ppermute(near, 'fft', [(f, f ^ 1) for f in range(BANDS)])  2.94 us
    pallas_call x1, Pallas kernels, pool(): pl.pallas_call(pool_kernel, out_shape=(jax.ShapeDtypeStruct((PAIRS * BLOC...  2.69 us
  transfers between devices with their start and end apart: 1, of which 1 were waited for; matrix products, arithmetic and copies ran while one was open for 0% of the time, Pallas kernels for 0%

profile of v2, /device:TPU:1, one launch (start us, length us, event | category | flops | bytes accessed | tf_op | source)
XLA Modules:
  0.0 69.9 jit_solution(12029416581099422274)
XLA Ops:
  0.7 0.0 copy-start.1
  0.7 0.7 copy-done.1
  1.3 2.7 %pool.1 = (f32[512,128]{1,0:T(8,128)S(1)}, s32[256,128]{1,0:T(8,128)S(1)}) custom-call(s32[1]{0:T(128)S(6)} %copy.11.count_ref, s32[1,256]{1,0:T(1,128)S(1)} %bitcast.13, bf16[256,4096]{1,0:T(8,128)(2,1)} %cot_hbm.1), custom_call_target="tpu_custom_call" | custom-call | tf_op jit(solution)/shard_map/pool/pallas_call | solution.py:180
  4.0 28.7 %all_to_all.16 = f32[128,4,128]{2,1,0:T(4,128)S(1)} all-to-all(f32[128,4,128]{2,1,0:T(4,128)S(1)} %bitcast.12), channel_id=1, replica_groups={{0,8,16,24,32,40,48,56,64,72,80,88,96,104,112,120,128,136,144,152,160,1..., dimensions={0} | all-to-all | bytes 524288 | tf_op jit(solution)/shard_map/all_to_all | solution.py:474
  32.7 2.9 %collective-permute-start = (f32[512,128]{1,0:T(8,128)S(1)}, f32[512,128]{1,0:T(8,128)S(1)}, u32[]{:S(2)}, u32[]{:S(2)}) collective-permute-start(f32[512,128]{1,0:T(8,128)S(1)} %bitcast.8), channel_id=1, source_target_pairs={{0,1},{1,0},{2,3},{3,2},{4,5},{5,4},{6,7},{7,6},{8,9},{9,8},{10,11... | collective-permute-start | bytes 786440 | tf_op jit(solution)/shard_map/ppermute | solution.py:484
  35.7 1.2 %collective-permute-done.pair_ref = f32[512,128]{1,0:T(8,128)S(1)} collective-permute-done((f32[512,128]{1,0:T(8,128)S(1)}, f32[512,128]{1,0:T(8,128)S(1)}, u32[]{:S(2)}, u32[]{:S(2)}) %collective-permute-start) | collective-permute-done | bytes 262176 | tf_op jit(solution)/shard_map/ppermute | solution.py:484
  36.8 0.0 copy-start
  36.8 11.8 %conv.1 = f32[256,128]{1,0:T(8,128)S(1)} custom-call(s32[1,1]{1,0:T(1,128)} %bitcast.1.f_ref, f32[512,128]{1,0:T(8,128)S(1)} %bitcast.9, f32[512,128]{1,0:T(8,128)S(1)} %collective-permute-done.pair_ref, bf16[8,4,1024,256]{3,2,1,0:T(8,128)(2,1)} %constant.12.clone.fwd_hbm, bf16[4,3,512,256]{3,2,1,0:T(8,128)(2,1)} %constant.13.clone.rfwd_hbm, ...), custom_call_target="tpu_custom_call" | custom-call | tf_op jit(solution)/shard_map/conv/pallas_call | solution.py:385
  48.6 18.0 %all_to_all.17 = f32[256,1,128]{2,1,0:T(1,128)S(1)} all-to-all(f32[256,1,128]{2,1,0:T(1,128)S(1)} %bitcast.10), channel_id=1, replica_groups=mesh['tiles'=32,'fft'=8] {'fft','tiles'}, dimensions={0} | all-to-all | bytes 262144 | tf_op jit(solution)/shard_map/all_to_all | solution.py:474
  66.6 0.0 copy-done
  66.6 3.2 %spread.1 = bf16[256,4096]{1,0:T(8,128)(2,1)} custom-call(s32[256,128]{1,0:T(8,128)S(1)} %get-tuple-element.7.meta_ref, f32[256,128]{1,0:T(8,128)S(1)} %bitcast.11, bf16[256,4096]{1,0:T(8,128)(2,1)S(1)} %copy-done), custom_call_target="tpu_custom_call" | custom-call | tf_op jit(solution)/shard_map/spread/pallas_call | solution.py:454
Async XLA Ops:
  0.7 0.7 copy-start.1
  32.7 4.1 %collective-permute-start = (f32[512,128]{1,0:T(8,128)S(1)}, f32[512,128]{1,0:T(8,128)S(1)}, u32[]{:S(2)}, u32[]{:S(2)}) collective-permute-start(f32[512,128]{1,0:T(8,128)S(1)} %bitcast.8), channel_id=1, source_target_pairs={{0,1},{1,0},{2,3},{3,2},{4,5},{5,4},{6,7},{7,6},{8,9},{9,8},{10,11... | collective-permute-start | bytes 786440 | tf_op jit(solution)/shard_map/ppermute | solution.py:484
  36.8 29.8 %copy-start = (bf16[256,4096]{1,0:T(8,128)(2,1)S(1)}, bf16[256,4096]{1,0:T(8,128)(2,1)}, u32[]{:S(2)}) copy-start(bf16[256,4096]{1,0:T(8,128)(2,1)} %base_hbm.1) | copy-start | bytes 6291460

commit v3 on v2

--- a/solution.py
+++ b/solution.py
@@ -66,7 +66,7 @@
         rows.append(np.block([[c, s], [-s, c]]))
     rows = np.stack(rows)
     both = np.stack(split_np(rows)).reshape(2, 4, 2, CHUNKS, STEP, 256)
-    rfwd = both.transpose(1, 3, 0, 2, 4, 5).reshape(4, CHUNKS, 4 * STEP, 256)
+    rfwd = both.transpose(1, 0, 3, 2, 4, 5).reshape(4, 2, 2 * PART0, 256)
     rback = np.concatenate(split_np(rows.transpose(0, 2, 1)), axis=1)
     return fwd, back, rfwd, rback
 
@@ -77,16 +77,13 @@
     return high, low
 
 
-def split3(x):
-    high = x.astype(BF)
-    rest = x - high.astype(F32)
-    mid = rest.astype(BF)
-    low = (rest - mid.astype(F32)).astype(BF)
-    return high, mid, low
-
-
 def dot(a, b):
     return jnp.dot(a, b, preferred_element_type=F32)
+
+
+def dot3(a_high, a_low, b_high, b_low):
+    left = jnp.concatenate([a_high, a_high, a_low], axis=1)
+    return dot(left, jnp.concatenate([b_high, b_low, b_high], axis=0))
 
 
 def dot_nt(a, b):
@@ -154,16 +151,15 @@
     for i in range(4):
         weights = jnp.where(match_j & ((plane & 3) == i), 1.0, 0.0).astype(BF)
         copies[i].wait()
-        for c in range(4):
-            total = total + dot(cot[:, i * 1024 + c * 256 : i * 1024 + (c + 1) * 256], weights)
+        total = total + dot(
+            cot[:, i * 1024 : (i + 1) * 1024], jnp.concatenate([weights] * 4, axis=0)
+        )
     plain, flipped = total[:, :128], total[:, 128:]
     here = (lane >> 4) == rank_col
     own = jnp.where(here, jnp.where(right_col, plain, flipped), 0.0)
     halo = jnp.where(here, jnp.where(right_col, flipped, plain), 0.0)
     loads = jnp.concatenate([own, halo, mark_own, mark_halo], axis=1)
-    out = jnp.zeros((3 * BLOCKS, 512), F32)
-    for piece in split3(loads):
-        out = out + dot(hot, piece)
+    out = dot(jnp.concatenate([hot, hot], axis=1), jnp.concatenate(split(loads), axis=0))
     lane32 = iota((BLOCKS, 128), 1)
     marks = jnp.where(
         lane32 < 8,
@@ -185,8 +181,8 @@
         ),
         in_specs=[
             pl.BlockSpec(memory_space=pltpu.SMEM),
-            pl.BlockSpec(memory_space=pl.ANY),
-            pl.BlockSpec(memory_space=pl.ANY),
+            pl.BlockSpec(memory_space=pltpu.HBM),
+            pl.BlockSpec(memory_space=pltpu.HBM),
         ],
         out_specs=(
             pl.BlockSpec(memory_space=pltpu.VMEM),
@@ -225,8 +221,7 @@
         pltpu.make_async_copy(rback_hbm, rback, sems.at[3]),
         pltpu.make_async_copy(back_hbm.at[f], back, sems.at[4]),
     ]
-    for copy in copies:
-        copy.start()
+    copies[0].start()
     core = f & 1
 
     lane16 = iota((16, 128), 1)
@@ -251,8 +246,9 @@
         return 2 * (spot & (PAIRS - 1)) + (core ^ (spot >> 2))
 
     def hot_of(code, rows):
-        place = jnp.broadcast_to(code[0:1, :] & 255, (rows, 256))
-        return jnp.where(iota((rows, 256), 0) == place, 1.0, 0.0).astype(BF)
+        place = jnp.broadcast_to(code[0:1, :] & 255, (rows, 256)).astype(jnp.int16)
+        hit = iota((rows, 256), 0).astype(jnp.int16) == place
+        return jnp.where(hit, jnp.ones((), BF), jnp.zeros((), BF))
 
     def scatter(spot, carry):
         base = pl.multiple_of(band_of(spot) * 16, 16)
@@ -263,15 +259,15 @@
             values = tv[spot, nbr]
             high = values.astype(BF).astype(F32)
             low = values - high
-            parts = []
+            sides = []
             for piece in (high, low):
-                for c in range(CELLS):
-                    parts.append(
-                        jnp.where(mask, jnp.broadcast_to(piece[c : c + 1, :], (16, 256)), 0.0).astype(BF)
-                    )
-            left = jnp.concatenate(parts, axis=0)
-            both = dot_nt(left, hot_of(code, 256 if nbr == 0 else 128))
-            outs.append(both[:256] + both[256:])
+                parts = [
+                    jnp.where(mask, jnp.broadcast_to(piece[c : c + 1, :], (16, 256)), 0.0).astype(BF)
+                    for c in range(CELLS)
+                ]
+                sides.append(jnp.concatenate(parts, axis=0))
+            hot = hot_of(code, 256 if nbr == 0 else 128)
+            outs.append(dot_nt(jnp.concatenate(sides, axis=1), jnp.concatenate([hot, hot], axis=1)))
         near_r, near_l = outs[0][:, :128], outs[0][:, 128:]
         far_l, far_r = outs[1], outs[2]
         for ref, near, far in ((e_s, near_r + near_l, far_r + far_l), (o_s, near_r - near_l, far_r - far_l)):
@@ -285,13 +281,15 @@
                             )
         return carry
 
+    copies[1].start()
+    copies[2].start()
     lax.fori_loop(0, BANDS, scatter, 0, unroll=UNROLL)
+    copies[3].start()
+    copies[4].start()
 
     copies[0].wait()
     for part, ref in enumerate((e_s, o_s)):
-        first = dot(ref[...], fwd[2 * part])
-        second = dot(ref[:ROWS, :], fwd[2 * part + 1])
-        y = first[:ROWS] + (first[ROWS:] + second)
+        y = dot3(ref[:ROWS, :], ref[ROWS:, :], fwd[2 * part], fwd[2 * part + 1])
         for level, piece in enumerate(split(y)):
             for i in range(4):
                 y_s[level, i, part * 128 : (part + 1) * 128, :] = piece[i * 128 : (i + 1) * 128]
@@ -309,9 +307,8 @@
 
     for chunk in range(CHUNKS):
         for i in range(4):
-            first = dot(rfwd[i, chunk], y_s[0, i])
-            second = dot(rfwd[i, chunk, : 2 * STEP, :], y_s[1, i])
-            g_s[chunk, i] = first[: 2 * STEP] + (first[2 * STEP :] + second)
+            rows = slice(chunk * 2 * STEP, (chunk + 1) * 2 * STEP)
+            g_s[chunk, i] = dot3(rfwd[i, 0, rows, :], rfwd[i, 1, rows, :], y_s[0, i], y_s[1, i])
         for r in range(0, STEP, 16):
             for lanes in (slice(0, 128), slice(128, 256)):
                 g = [(g_s[chunk, i, r : r + 16, lanes], g_s[chunk, i, STEP + r : STEP + r + 16, lanes])
@@ -329,37 +326,39 @@
 
     copies[3].wait()
     for i in range(4):
-        first = dot(rback[i], q_s[0, i])
-        second = dot(rback[i, :256, :], q_s[1, i])
-        z = first[:256] + (first[256:] + second)
+        z = dot3(rback[i, :256, :], rback[i, 256:, :], q_s[0, i], q_s[1, i])
         for level, piece in enumerate(split(z)):
             for part in range(2):
                 z_s[part, level * ROWS + i * 128 : level * ROWS + (i + 1) * 128, :] = (
                     piece[part * 128 : (part + 1) * 128]
                 )
     copies[4].wait()
-    for j in range(4):
-        lanes = slice(j * 128, (j + 1) * 128)
+    for jj in range(2):
+        lanes = slice(jj * 256, (jj + 1) * 256)
         sums = []
         for part in range(2):
-            first = dot(z_s[part], back[2 * part, :, lanes])
-            second = dot(z_s[part, :ROWS, :], back[2 * part + 1, :, lanes])
-            sums.append(first[:ROWS] + (first[ROWS:] + second))
+            sums.append(
+                dot3(z_s[part, :ROWS, :], z_s[part, ROWS:, :], back[2 * part, :, lanes], back[2 * part + 1, :, lanes])
+            )
         for side, value in enumerate((sums[0] - sums[1], sums[0] + sums[1])):
             for level, piece in enumerate(split(value)):
-                s_s[level, j, :, side * 128 : (side + 1) * 128] = piece
+                for j in range(2):
+                    s_s[level, 2 * jj + j, :, side * 128 : (side + 1) * 128] = (
+                        piece[:, j * 128 : (j + 1) * 128]
+                    )
 
     def gather(spot, carry):
         base = pl.multiple_of(band_of(spot) * 16, 16)
         code = tm[spot, 0]
         hot = hot_of(code, 256)
         mask = row16 == jnp.broadcast_to(code[0:1, :] >> 8, (16, 256))
-        left = jnp.concatenate(
-            [s_s[level, j, pl.ds(i * 128 + base, 16), :] for level in range(2) for j in range(4) for i in range(4)],
-            axis=0,
-        )
-        both = dot(left, hot)
-        total = both[:256] + both[256:]
+        left = [
+            jnp.concatenate(
+                [s_s[level, j, pl.ds(i * 128 + base, 16), :] for j in range(4) for i in range(4)], axis=0
+            )
+            for level in range(2)
+        ]
+        total = dot(jnp.concatenate(left, axis=1), jnp.concatenate([hot, hot], axis=0))
         for c in range(CELLS):
             tg[spot, c : c + 1, :] = jnp.sum(
                 jnp.where(mask, total[c * 16 : (c + 1) * 16, :], 0.0), axis=0, keepdims=True
@@ -392,7 +391,7 @@
         out_specs=vmem_spec,
         scratch_shapes=[
             pltpu.VMEM((4, 1024, STRIP), BF),
-            pltpu.VMEM((4, CHUNKS, 4 * STEP, 256), BF),
+            pltpu.VMEM((4, 2, 2 * PART0, 256), BF),
             pltpu.VMEM((2, L0, STRIP), F32),
             pltpu.VMEM((4, 512, 2 * PART0), BF),
             pltpu.VMEM((4, STRIP, 512), BF),
@@ -413,58 +412,47 @@
     )(strip, near, pair, jnp.asarray(fwd), jnp.asarray(rfwd), psf, jnp.asarray(rback), jnp.asarray(back))
 
 
-def spread_kernel(meta_ref, back_ref, base_hbm, out_hbm, base, done, sems):
-    loads, stores = [], []
-    for i in range(4):
-        lanes = pl.ds(i * 1024, 1024)
-        loads.append(pltpu.make_async_copy(base_hbm.at[:, lanes], base.at[:, lanes], sems.at[i]))
-        stores.append(pltpu.make_async_copy(done.at[:, lanes], out_hbm.at[:, lanes], sems.at[4 + i]))
-    for load in loads:
-        load.start()
+def spread_kernel(meta_ref, back_ref, base_ref, out_hbm, done, sems):
     summed = back_ref[0:BLOCKS, :]
     for f in range(1, BANDS):
         summed = summed + back_ref[f * BLOCKS : (f + 1) * BLOCKS, :]
     meta = meta_ref[...]
     target, rank, right = meta[:, 0:1], meta[:, 1:2], meta[:, 2:3]
-    hot = jnp.where(iota((SLOTS, BLOCKS), 1) == target, 1.0, 0.0).astype(BF)
-    picked = jnp.zeros((SLOTS, 128), F32)
-    for piece in split3(summed):
-        picked = picked + dot(hot, piece)
+    lane64 = iota((SLOTS, 2 * BLOCKS), 1) & (BLOCKS - 1)
+    hot = jnp.where(lane64 == target, 1.0, 0.0).astype(BF)
+    picked = dot(hot, jnp.concatenate(split(summed), axis=0))
     lane = iota((SLOTS, 128), 1)
     picked = jnp.where((lane >> 4) == rank, picked, 0.0)
     plain = jnp.where(right == 1, picked, 0.0)
-    sides = split3(jnp.concatenate([plain, picked - plain], axis=1))
-    krow, nlane = iota((256, 128), 0), iota((256, 128), 1)
+    sides = jnp.concatenate(split(plain) + split(picked - plain), axis=1)
+    krow, nlane = iota((512, 128), 0), iota((512, 128), 1)
     have_j = (krow >> 2) & 3
-    have_j = jnp.where(krow >= 128, 3 - have_j, have_j)
+    have_j = jnp.where(krow >= 256, 3 - have_j, have_j)
     match = have_j == ((nlane >> 4) & 3)
+    stores = []
     for i in range(4):
-        weights = jnp.where(match & ((krow & 3) == i), 1.0, 0.0).astype(BF)
-        value = dot(sides[0], weights) + (dot(sides[1], weights) + dot(sides[2], weights))
-        loads[i].wait()
-        for m in range(8):
-            spot = slice(i * 1024 + m * 128, i * 1024 + (m + 1) * 128)
-            done[:, spot] = (base[:, spot].astype(F32) + value).astype(BF)
-        stores[i].start()
+        value = dot(sides, jnp.where(match & ((krow & 3) == i), 1.0, 0.0).astype(BF))
+        for h in range(2):
+            for m in range(4):
+                at = i * 1024 + h * 512 + m * 128
+                done[:, at : at + 128] = (base_ref[:, at : at + 128].astype(F32) + value).astype(BF)
+            lanes = pl.ds(i * 1024 + h * 512, 512)
+            stores.append(
+                pltpu.make_async_copy(done.at[:, lanes], out_hbm.at[:, lanes], sems.at[2 * i + h])
+            )
+            stores[-1].start()
     for store in stores:
         store.wait()
 
 
 def spread(meta, returned, base_grad):
+    vmem_spec = pl.BlockSpec(memory_space=pltpu.VMEM)
     return pl.pallas_call(
         spread_kernel,
         out_shape=jax.ShapeDtypeStruct((SLOTS, 4096), BF),
-        in_specs=[
-            pl.BlockSpec(memory_space=pltpu.VMEM),
-            pl.BlockSpec(memory_space=pltpu.VMEM),
-            pl.BlockSpec(memory_space=pl.ANY),
-        ],
-        out_specs=pl.BlockSpec(memory_space=pl.ANY),
-        scratch_shapes=[
-            pltpu.VMEM((SLOTS, 4096), BF),
-            pltpu.VMEM((SLOTS, 4096), BF),
-            pltpu.SemaphoreType.DMA((8,)),
-        ],
+        in_specs=[vmem_spec, vmem_spec, vmem_spec],
+        out_specs=pl.BlockSpec(memory_space=pltpu.HBM),
+        scratch_shapes=[pltpu.VMEM((SLOTS, 4096), BF), pltpu.SemaphoreType.DMA((8,))],
         compiler_params=pltpu.CompilerParams(vmem_limit_bytes=16 * 1024 * 1024),
         name="spread",
     )(meta, returned, base_grad)

time: 70.1 us -> 67.9 us (0.969)
  Pallas kernels: 17.6 us -> 15.8 us
    pallas_call x1, Pallas kernels: 3.16 us -> 1.89 us  [spread(): pl.pallas_call(spread_kernel, out_shape=jax.ShapeDtypeStruct((SLOTS, 4096...]
    pallas_call x1, Pallas kernels: 11.8 us -> 11.1 us  [conv(): pl.pallas_call(conv_kernel, out_shape=jax.ShapeDtypeStruct((BANDS * BLOCK...]
where the time goes in v3:
time: 67.9 us; the launch traced here: 67.7 us
  blocking collectives  46.5 us (68%)
  Pallas kernels  15.8 us (23%)
  starting transfers between devices  2.94 us (4%)
  waiting for transfers between devices  1.16 us (2%)
  local copies, waits for them, and re-layouts  0.68 us (1%)
  between operations  0.68 us (1%)
    all_to_all x2, blocking collectives, exchange(): lax.all_to_all(x, ('fft', 'tiles'), split_axis=0, concat_axis=0, axis_ind...  46.5 us
    pallas_call x1, Pallas kernels, conv(): pl.pallas_call(conv_kernel, out_shape=jax.ShapeDtypeStruct((BANDS * BLOCK...  11.1 us
    ppermute x1, starting transfers between devices, local(): pair = lax.ppermute(near, 'fft', [(f, f ^ 1) for f in range(BANDS)])  2.94 us
    pallas_call x1, Pallas kernels, pool(): pl.pallas_call(pool_kernel, out_shape=(jax.ShapeDtypeStruct((PAIRS * BLOC...  2.83 us
    pallas_call x1, Pallas kernels, spread(): pl.pallas_call(spread_kernel, out_shape=jax.ShapeDtypeStruct((SLOTS, 4096...  1.89 us
  transfers between devices with their start and end apart: 1, of which 1 were waited for; matrix products, arithmetic and copies ran while one was open for 0% of the time, Pallas kernels for 0%

profile of v3, /device:TPU:1, one launch (start us, length us, event | category | flops | bytes accessed | tf_op | source)
XLA Modules:
  0.0 67.7 jit_solution(10887406635496837888)
XLA Ops:
  0.7 0.0 copy-start.1
  0.7 0.7 copy-done.1
  1.3 2.8 %pool.1 = (f32[512,128]{1,0:T(8,128)S(1)}, s32[256,128]{1,0:T(8,128)S(1)}) custom-call(s32[1]{0:T(128)S(6)} %copy.11.count_ref, s32[1,256]{1,0:T(1,128)S(1)} %bitcast.13, bf16[256,4096]{1,0:T(8,128)(2,1)} %cot_hbm.1), custom_call_target="tpu_custom_call" | custom-call | tf_op jit(solution)/shard_map/pool/pallas_call | solution.py:176
  4.2 28.7 %all_to_all.16 = f32[128,4,128]{2,1,0:T(4,128)S(1)} all-to-all(f32[128,4,128]{2,1,0:T(4,128)S(1)} %bitcast.12), channel_id=1, replica_groups={{0,8,16,24,32,40,48,56,64,72,80,88,96,104,112,120,128,136,144,152,160,1..., dimensions={0} | all-to-all | bytes 524288 | tf_op jit(solution)/shard_map/all_to_all | solution.py:462
  32.9 2.9 %collective-permute-start = (f32[512,128]{1,0:T(8,128)S(1)}, f32[512,128]{1,0:T(8,128)S(1)}, u32[]{:S(2)}, u32[]{:S(2)}) collective-permute-start(f32[512,128]{1,0:T(8,128)S(1)} %bitcast.8), channel_id=1, source_target_pairs={{0,1},{1,0},{2,3},{3,2},{4,5},{5,4},{6,7},{7,6},{8,9},{9,8},{10,11... | collective-permute-start | bytes 786440 | tf_op jit(solution)/shard_map/ppermute | solution.py:472
  35.8 1.2 %collective-permute-done.pair_ref = f32[512,128]{1,0:T(8,128)S(1)} collective-permute-done((f32[512,128]{1,0:T(8,128)S(1)}, f32[512,128]{1,0:T(8,128)S(1)}, u32[]{:S(2)}, u32[]{:S(2)}) %collective-permute-start) | collective-permute-done | bytes 262176 | tf_op jit(solution)/shard_map/ppermute | solution.py:472
  37.0 0.0 copy-start
  37.0 11.1 %conv.1 = f32[256,128]{1,0:T(8,128)S(1)} custom-call(s32[1,1]{1,0:T(1,128)} %bitcast.1.f_ref, f32[512,128]{1,0:T(8,128)S(1)} %bitcast.9, f32[512,128]{1,0:T(8,128)S(1)} %collective-permute-done.pair_ref, bf16[8,4,1024,256]{3,2,1,0:T(8,128)(2,1)} %constant.12.clone.fwd_hbm, bf16[4,2,768,256]{3,2,1,0:T(8,128)(2,1)} %constant.13.clone.rfwd_hbm, ...), custom_call_target="tpu_custom_call" | custom-call | tf_op jit(solution)/shard_map/conv/pallas_call | solution.py:384
  48.0 17.8 %all_to_all.17 = f32[256,1,128]{2,1,0:T(1,128)S(1)} all-to-all(f32[256,1,128]{2,1,0:T(1,128)S(1)} %bitcast.10), channel_id=1, replica_groups=mesh['tiles'=32,'fft'=8] {'fft','tiles'}, dimensions={0} | all-to-all | bytes 262144 | tf_op jit(solution)/shard_map/all_to_all | solution.py:462
  65.9 0.0 copy-done
  65.9 1.9 %spread.1 = bf16[256,4096]{1,0:T(8,128)(2,1)} custom-call(s32[256,128]{1,0:T(8,128)S(1)} %get-tuple-element.7.meta_ref, f32[256,128]{1,0:T(8,128)S(1)} %bitcast.11, bf16[256,4096]{1,0:T(8,128)(2,1)S(1)} %copy-done), custom_call_target="tpu_custom_call" | custom-call | tf_op jit(solution)/shard_map/spread/pallas_call | solution.py:450
Async XLA Ops:
  0.7 0.7 %copy-start.1 = (s32[256]{0:T(256)S(1)}, s32[256]{0:T(256)}, u32[]{:S(2)}) copy-start(s32[256]{0:T(256)} %param.11) | copy-start | bytes 3076
  32.9 4.1 %collective-permute-start = (f32[512,128]{1,0:T(8,128)S(1)}, f32[512,128]{1,0:T(8,128)S(1)}, u32[]{:S(2)}, u32[]{:S(2)}) collective-permute-start(f32[512,128]{1,0:T(8,128)S(1)} %bitcast.8), channel_id=1, source_target_pairs={{0,1},{1,0},{2,3},{3,2},{4,5},{5,4},{6,7},{7,6},{8,9},{9,8},{10,11... | collective-permute-start | bytes 786440 | tf_op jit(solution)/shard_map/ppermute | solution.py:472
  37.0 28.9 %copy-start = (bf16[256,4096]{1,0:T(8,128)(2,1)S(1)}, bf16[256,4096]{1,0:T(8,128)(2,1)}, u32[]{:S(2)}) copy-start(bf16[256,4096]{1,0:T(8,128)(2,1)} %base_ref.1) | copy-start | bytes 6291460

commit v4 on v3

--- a/solution.py
+++ b/solution.py
@@ -30,8 +30,7 @@
 PAIRS = BANDS // 2
 BF = jnp.bfloat16
 F32 = jnp.float32
-UNROLL = 4
-VMEM_LIMIT = 52 * 1024 * 1024
+VMEM_LIMIT = 48 * 1024 * 1024
 
 
 def split_np(table):
@@ -59,15 +58,20 @@
     sh, sl = split_np(strips(sin[near]).transpose(0, 2, 1) * scale)
     back = np.stack([ch, cl, sh, sl], axis=1)
     k0 = np.arange(PART0)
-    rows = []
-    for i in range(4):
-        angle = (np.outer(k0, 4 * np.arange(128) + i) % L0) * (2 * math.pi / L0)
-        c, s = np.cos(angle), np.sin(angle)
-        rows.append(np.block([[c, s], [-s, c]]))
-    rows = np.stack(rows)
-    both = np.stack(split_np(rows)).reshape(2, 4, 2, CHUNKS, STEP, 256)
-    rfwd = both.transpose(1, 0, 3, 2, 4, 5).reshape(4, 2, 2 * PART0, 256)
-    rback = np.concatenate(split_np(rows.transpose(0, 2, 1)), axis=1)
+    rfwd, rback = [], []
+    for core in range(2):
+        bands = np.r_[core:BANDS:2, 1 - core : BANDS : 2]
+        tile_row = (bands[:, None] * TILE_ROWS + np.arange(TILE_ROWS)).reshape(-1)
+        rows = []
+        for i in range(4):
+            angle = (np.outer(k0, 4 * tile_row + i) % L0) * (2 * math.pi / L0)
+            c, s = np.cos(angle), np.sin(angle)
+            rows.append(np.block([[c, s], [-s, c]]))
+        rows = np.stack(rows)
+        both = np.stack(split_np(rows)).reshape(2, 4, 2, CHUNKS, STEP, 256)
+        rfwd.append(both.transpose(1, 0, 3, 2, 4, 5).reshape(4, 2, 2 * PART0, 256))
+        rback.append(np.concatenate(split_np(rows.transpose(0, 2, 1)), axis=1))
+    rfwd, rback = np.stack(rfwd), np.stack(rback)
     return fwd, back, rfwd, rback
 
 
@@ -94,9 +98,7 @@
     return lax.broadcasted_iota(jnp.int32, shape, dim)
 
 
-def pool_kernel(count_ref, place_hbm, cot_hbm, msg_ref, meta_ref, place_ref, cot, sems):
-    fetch = pltpu.make_async_copy(place_hbm, place_ref, sems.at[4])
-    fetch.start()
+def pool_kernel(place_ref, cot_hbm, msg_ref, meta_ref, cot, sems):
     copies = [
         pltpu.make_async_copy(
             cot_hbm.at[:, pl.ds(i * 1024, 1024)], cot.at[:, pl.ds(i * 1024, 1024)], sems.at[i]
@@ -105,8 +107,6 @@
     ]
     for copy in copies:
         copy.start()
-    count = count_ref[0]
-    fetch.wait()
     place_row = place_ref[...]
     square = (SLOTS, SLOTS)
     down, across = iota(square, 0), iota(square, 1)
@@ -117,12 +117,12 @@
         target = jnp.where(live, column >> 8, -8)
         return row, target, column & (TILE_COLS - 1)
 
-    live_row = iota((1, SLOTS), 1) < count
+    live_row = place_row >= 0
     _, target_row, tc_row = fields(place_row, live_row)
     place_col = jnp.sum(
         jnp.where(down == across, place_row.astype(F32), 0.0), axis=1, keepdims=True
     ).astype(jnp.int32)
-    live_col = iota((SLOTS, 1), 0) < count
+    live_col = place_col >= 0
     tr_col, target_col, tc_col = fields(place_col, live_col)
     before = (target_row == target_col) & (across < down) & live_row
     rank_col = jnp.sum(jnp.where(before, 1.0, 0.0), axis=1, keepdims=True).astype(jnp.int32)
@@ -173,6 +173,7 @@
 
 
 def pool(cotangent, tile_place, tile_count):
+    live_place = jnp.where(jnp.arange(SLOTS, dtype=jnp.int32) < tile_count[0], tile_place, -1)
     return pl.pallas_call(
         pool_kernel,
         out_shape=(
@@ -180,22 +181,20 @@
             jax.ShapeDtypeStruct((SLOTS, 128), jnp.int32),
         ),
         in_specs=[
-            pl.BlockSpec(memory_space=pltpu.SMEM),
-            pl.BlockSpec(memory_space=pltpu.HBM),
-            pl.BlockSpec(memory_space=pltpu.HBM),
+            pl.BlockSpec(memory_space=pltpu.VMEM),
+            pl.BlockSpec(memory_space=pl.ANY),
         ],
         out_specs=(
             pl.BlockSpec(memory_space=pltpu.VMEM),
             pl.BlockSpec(memory_space=pltpu.VMEM),
         ),
         scratch_shapes=[
-            pltpu.VMEM((1, SLOTS), jnp.int32),
             pltpu.VMEM((SLOTS, 4096), BF),
-            pltpu.SemaphoreType.DMA((5,)),
+            pltpu.SemaphoreType.DMA((4,)),
         ],
         compiler_params=pltpu.CompilerParams(vmem_limit_bytes=VMEM_LIMIT),
         name="pool",
-    )(tile_count, tile_place.reshape(1, SLOTS), cotangent)
+    )(live_place.reshape(1, SLOTS), cotangent)
 
 
 def chunk_swap(pieces, lane):
@@ -209,54 +208,37 @@
     return out
 
 
-def conv_kernel(
-    f_ref, near_ref, pair_ref, fwd_hbm, rfwd_hbm, psf_hbm, rback_hbm, back_hbm, out_ref,
-    fwd, rfwd, psf, rback, back, tv, tm, e_s, o_s, y_s, g_s, q_s, z_s, s_s, tg, sems,
-):
-    f = f_ref[0, 0]
-    copies = [
-        pltpu.make_async_copy(fwd_hbm.at[f], fwd, sems.at[0]),
-        pltpu.make_async_copy(rfwd_hbm, rfwd, sems.at[1]),
-        pltpu.make_async_copy(psf_hbm, psf, sems.at[2]),
-        pltpu.make_async_copy(rback_hbm, rback, sems.at[3]),
-        pltpu.make_async_copy(back_hbm.at[f], back, sems.at[4]),
-    ]
-    copies[0].start()
-    core = f & 1
-
+def arrive(ref, tv, tm):
     lane16 = iota((16, 128), 1)
     lane8 = iota((8, 128), 1)
-    for half, ref in enumerate((near_ref, pair_ref)):
-        turned = [jnp.transpose(ref[pl.ds(a, 128, stride=4), :]) for a in range(4)]
-        for nbr in range(3):
-            for eh in range(2):
-                group = [turned[nbr][(eh * 4 + e) * 16 : (eh * 4 + e + 1) * 16, :] for e in range(4)]
-                for x, value in enumerate(chunk_swap(group, lane16)):
-                    tv[half * PAIRS + x, nbr, :, eh * 128 : (eh + 1) * 128] = value
-                marks = turned[3][nbr * 8 : nbr * 8 + 8, :]
-                group = [
-                    jnp.broadcast_to(marks[eh * 4 + e : eh * 4 + e + 1, :], (8, 128)) for e in range(4)
-                ]
-                for x, value in enumerate(chunk_swap(group, lane8)):
-                    tm[half * PAIRS + x, nbr, :, eh * 128 : (eh + 1) * 128] = value.astype(jnp.int32) - 1
-
+    turned = [jnp.transpose(ref[pl.ds(a, 128, stride=4), :]) for a in range(4)]
+    for nbr in range(3):
+        for eh in range(2):
+            group = [turned[nbr][(eh * 4 + e) * 16 : (eh * 4 + e + 1) * 16, :] for e in range(4)]
+            for x, value in enumerate(chunk_swap(group, lane16)):
+                tv[x, nbr, :, eh * 128 : (eh + 1) * 128] = value
+            marks = turned[3][nbr * 8 : nbr * 8 + 8, :]
+            group = [jnp.broadcast_to(marks[eh * 4 + e : eh * 4 + e + 1, :], (8, 128)) for e in range(4)]
+            for x, value in enumerate(chunk_swap(group, lane8)):
+                tm[x, nbr, :, eh * 128 : (eh + 1) * 128] = value.astype(jnp.int32) - 1
+
+
+def hot_of(code, rows):
+    place = jnp.broadcast_to(code[0:1, :] & 255, (rows, 256)).astype(jnp.int16)
+    hit = iota((rows, 256), 0).astype(jnp.int16) == place
+    return jnp.where(hit, jnp.ones((), BF), jnp.zeros((), BF))
+
+
+def scatter(tv, tm, planes):
     row16 = iota((16, 256), 0)
 
-    def band_of(spot):
-        return 2 * (spot & (PAIRS - 1)) + (core ^ (spot >> 2))
-
-    def hot_of(code, rows):
-        place = jnp.broadcast_to(code[0:1, :] & 255, (rows, 256)).astype(jnp.int16)
-        hit = iota((rows, 256), 0).astype(jnp.int16) == place
-        return jnp.where(hit, jnp.ones((), BF), jnp.zeros((), BF))
-
-    def scatter(spot, carry):
-        base = pl.multiple_of(band_of(spot) * 16, 16)
+    def one(x, carry):
+        base = pl.multiple_of(x * 16, 16)
         outs = []
         for nbr in range(3):
-            code = tm[spot, nbr]
+            code = tm[x, nbr]
             mask = row16 == jnp.broadcast_to(code[0:1, :] >> 8, (16, 256))
-            values = tv[spot, nbr]
+            values = tv[x, nbr]
             high = values.astype(BF).astype(F32)
             low = values - high
             sides = []
@@ -270,29 +252,79 @@
             outs.append(dot_nt(jnp.concatenate(sides, axis=1), jnp.concatenate([hot, hot], axis=1)))
         near_r, near_l = outs[0][:, :128], outs[0][:, 128:]
         far_l, far_r = outs[1], outs[2]
-        for ref, near, far in ((e_s, near_r + near_l, far_r + far_l), (o_s, near_r - near_l, far_r - far_l)):
+        for kind, near, far in ((0, near_r + near_l, far_r + far_l), (1, near_r - near_l, far_r - far_l)):
             for part, value in enumerate((near, far)):
                 for level, piece in enumerate(split(value)):
                     for j in range(4):
                         for i in range(4):
-                            ref[pl.ds(level * ROWS + i * 128 + base, 16),
-                                j * 256 + part * 128 : j * 256 + (part + 1) * 128] = (
+                            planes[kind, pl.ds(level * 256 + i * 64 + base, 16),
+                                   j * 256 + part * 128 : j * 256 + (part + 1) * 128] = (
                                 piece[(j * 4 + i) * 16 : (j * 4 + i + 1) * 16, :]
                             )
         return carry
 
+    lax.fori_loop(0, PAIRS, one, 0, unroll=PAIRS)
+
+
+def first_kernel(near_ref, planes_ref, codes_ref, tv, tm):
+    arrive(near_ref, tv, tm)
+    codes_ref[...] = tm[:, 0]
+    scatter(tv, tm, planes_ref)
+
+
+def first(near):
+    vmem_spec = pl.BlockSpec(memory_space=pltpu.VMEM)
+    return pl.pallas_call(
+        first_kernel,
+        out_shape=(
+            jax.ShapeDtypeStruct((2, ROWS, 1024), BF),
+            jax.ShapeDtypeStruct((PAIRS, 8, 256), jnp.int32),
+        ),
+        in_specs=[vmem_spec],
+        out_specs=(vmem_spec, vmem_spec),
+        scratch_shapes=[
+            pltpu.VMEM((PAIRS, 3, CELLS, 256), F32),
+            pltpu.VMEM((PAIRS, 3, 8, 256), jnp.int32),
+        ],
+        compiler_params=pltpu.CompilerParams(vmem_limit_bytes=16 * 1024 * 1024),
+        cost_estimate=pl.CostEstimate(flops=2 * 10**9, bytes_accessed=4 * 10**6, transcendentals=0),
+        name="first",
+    )(near)
+
+
+def conv_kernel(
+    planes_ref, codes_ref, pair_ref, fwd_hbm, rfwd_hbm, psf_hbm, rback_hbm, back_hbm, out_ref,
+    fwd, rfwd, psf, rback, back, tv, tm, planes, y_s, g_s, q_s, z_s, s_s, tg, sems,
+):
+    f = lax.axis_index("fft")
+    core = f & 1
+    copies = [
+        pltpu.make_async_copy(fwd_hbm.at[f], fwd, sems.at[0]),
+        pltpu.make_async_copy(rfwd_hbm.at[core], rfwd, sems.at[1]),
+        pltpu.make_async_copy(psf_hbm, psf, sems.at[2]),
+        pltpu.make_async_copy(rback_hbm.at[core], rback, sems.at[3]),
+        pltpu.make_async_copy(back_hbm.at[f], back, sems.at[4]),
+    ]
+    copies[0].start()
+    arrive(pair_ref, tv, tm)
     copies[1].start()
     copies[2].start()
-    lax.fori_loop(0, BANDS, scatter, 0, unroll=UNROLL)
+    scatter(tv, tm, planes)
     copies[3].start()
     copies[4].start()
 
     copies[0].wait()
-    for part, ref in enumerate((e_s, o_s)):
-        y = dot3(ref[:ROWS, :], ref[ROWS:, :], fwd[2 * part], fwd[2 * part + 1])
+    for part in range(2):
+        high, low = [
+            jnp.concatenate([ref[part, level * 256 : (level + 1) * 256, :] for ref in (planes_ref, planes)], axis=0)
+            for level in range(2)
+        ]
+        y = dot3(high, low, fwd[2 * part], fwd[2 * part + 1])
         for level, piece in enumerate(split(y)):
             for i in range(4):
-                y_s[level, i, part * 128 : (part + 1) * 128, :] = piece[i * 128 : (i + 1) * 128]
+                for half in range(2):
+                    at = part * 128 + half * 64
+                    y_s[level, i, at : at + 64, :] = piece[half * 256 + i * 64 : half * 256 + (i + 1) * 64]
 
     copies[1].wait()
     copies[2].wait()
@@ -347,37 +379,42 @@
                         piece[:, j * 128 : (j + 1) * 128]
                     )
 
-    def gather(spot, carry):
-        base = pl.multiple_of(band_of(spot) * 16, 16)
-        code = tm[spot, 0]
-        hot = hot_of(code, 256)
-        mask = row16 == jnp.broadcast_to(code[0:1, :] >> 8, (16, 256))
-        left = [
-            jnp.concatenate(
-                [s_s[level, j, pl.ds(i * 128 + base, 16), :] for j in range(4) for i in range(4)], axis=0
-            )
-            for level in range(2)
-        ]
-        total = dot(jnp.concatenate(left, axis=1), jnp.concatenate([hot, hot], axis=0))
-        for c in range(CELLS):
-            tg[spot, c : c + 1, :] = jnp.sum(
-                jnp.where(mask, total[c * 16 : (c + 1) * 16, :], 0.0), axis=0, keepdims=True
-            )
-        return carry
-
-    lax.fori_loop(0, BANDS, gather, 0, unroll=UNROLL)
+    row16 = iota((16, 256), 0)
+    for half in range(2):
+
+        def gather(x, carry, half=half):
+            base = pl.multiple_of(half * 64 + x * 16, 16)
+            code = codes_ref[x] if half == 0 else tm[x, 0]
+            hot = hot_of(code, 256)
+            mask = row16 == jnp.broadcast_to(code[0:1, :] >> 8, (16, 256))
+            left = [
+                jnp.concatenate(
+                    [s_s[level, j, pl.ds(i * 128 + base, 16), :] for j in range(4) for i in range(4)], axis=0
+                )
+                for level in range(2)
+            ]
+            total = dot(jnp.concatenate(left, axis=1), jnp.concatenate([hot, hot], axis=0))
+            for c in range(CELLS):
+                tg[half, x, c : c + 1, :] = jnp.sum(
+                    jnp.where(mask, total[c * 16 : (c + 1) * 16, :], 0.0), axis=0, keepdims=True
+                )
+            return carry
+
+        lax.fori_loop(0, PAIRS, gather, 0, unroll=PAIRS)
+
+    lane16 = iota((16, 128), 1)
     for half in range(2):
         pieces = []
         for eh in range(2):
-            group = [tg[half * PAIRS + x, :, eh * 128 : (eh + 1) * 128] for x in range(4)]
+            group = [tg[half, x, :, eh * 128 : (eh + 1) * 128] for x in range(4)]
             pieces += chunk_swap(group, lane16)
         turned = jnp.transpose(jnp.concatenate(pieces, axis=0))
         for x in range(PAIRS):
-            base = pl.multiple_of(band_of(half * PAIRS + x) * BLOCKS, BLOCKS)
+            base = pl.multiple_of((2 * x + (core ^ half)) * BLOCKS, BLOCKS)
             out_ref[pl.ds(base, BLOCKS), :] = turned[x * BLOCKS : (x + 1) * BLOCKS, :]
 
 
-def conv(strip, near, pair, psf):
+def conv(planes, codes, pair, psf):
     fwd, back, rfwd, rback = tables()
     any_spec = pl.BlockSpec(memory_space=pl.ANY)
     vmem_spec = pl.BlockSpec(memory_space=pltpu.VMEM)
@@ -385,7 +422,7 @@
         conv_kernel,
         out_shape=jax.ShapeDtypeStruct((BANDS * BLOCKS, 128), F32),
         in_specs=[
-            pl.BlockSpec(memory_space=pltpu.SMEM), vmem_spec, vmem_spec,
+            vmem_spec, vmem_spec, vmem_spec,
             any_spec, any_spec, any_spec, any_spec, any_spec,
         ],
         out_specs=vmem_spec,
@@ -395,21 +432,20 @@
             pltpu.VMEM((2, L0, STRIP), F32),
             pltpu.VMEM((4, 512, 2 * PART0), BF),
             pltpu.VMEM((4, STRIP, 512), BF),
-            pltpu.VMEM((BANDS, 3, CELLS, 256), F32),
-            pltpu.VMEM((BANDS, 3, 8, 256), jnp.int32),
-            pltpu.VMEM((2 * ROWS, 1024), BF),
-            pltpu.VMEM((2 * ROWS, 1024), BF),
+            pltpu.VMEM((PAIRS, 3, CELLS, 256), F32),
+            pltpu.VMEM((PAIRS, 3, 8, 256), jnp.int32),
+            pltpu.VMEM((2, ROWS, 1024), BF),
             pltpu.VMEM((2, 4, 256, STRIP), BF),
             pltpu.VMEM((CHUNKS, 4, 2 * STEP, STRIP), F32),
             pltpu.VMEM((2, 4, 2 * PART0, STRIP), BF),
             pltpu.VMEM((2, 2 * ROWS, STRIP), BF),
             pltpu.VMEM((2, 4, ROWS, 256), BF),
-            pltpu.VMEM((BANDS, CELLS, 256), F32),
+            pltpu.VMEM((2, PAIRS, CELLS, 256), F32),
             pltpu.SemaphoreType.DMA((5,)),
         ],
         compiler_params=pltpu.CompilerParams(vmem_limit_bytes=VMEM_LIMIT),
         name="conv",
-    )(strip, near, pair, jnp.asarray(fwd), jnp.asarray(rfwd), psf, jnp.asarray(rback), jnp.asarray(back))
+    )(planes, codes, pair, jnp.asarray(fwd), jnp.asarray(rfwd), psf, jnp.asarray(rback), jnp.asarray(back))
 
 
 def spread_kernel(meta_ref, back_ref, base_ref, out_hbm, done, sems):
@@ -465,12 +501,12 @@
 
 
 def local(cotangent, base_grad, tile_place, tile_count, psf_spectrum):
-    strip = lax.axis_index("fft").astype(jnp.int32).reshape(1, 1)
     message, meta = pool(cotangent, tile_place, tile_count)
     groups = [[f * BLOCKS + t for f in range(c, BANDS, 2) for t in range(BLOCKS)] for c in range(2)]
     near = exchange(message.reshape(PAIRS * BLOCKS, 4, 128), groups).reshape(-1, 128)
     pair = lax.ppermute(near, "fft", [(f, f ^ 1) for f in range(BANDS)])
-    partial = conv(strip, near, pair, psf_spectrum)
+    planes, codes = first(near)
+    partial = conv(planes, codes, pair, psf_spectrum)
     returned = exchange(partial)
     return spread(meta, returned, base_grad)
 

time: 67.9 us -> 67.6 us (level)
  waiting for transfers between devices: 1.16 us -> 0.01 us
  Pallas kernels: 15.8 us -> 14.7 us
  local copies, waits for them, and re-layouts: 0.68 us -> 1.6 us
  other arithmetic: 0 us -> 0.68 us
    pallas_call x1, Pallas kernels: 11.1 us -> 9.3 us  [conv(): pl.pallas_call(conv_kernel, out_shape=jax.ShapeDtypeStruct((BANDS * BLOCK...]
    pallas_call x0 -> x1, Pallas kernels: none -> 1.35 us  [first(): pl.pallas_call(first_kernel, out_shape=(jax.ShapeDtypeStruct((2, ROWS, 10...]
    ppermute x1, waiting for transfers between devices: 1.16 us -> 0.01 us  [local(): pair = lax.ppermute(near, 'fft', [(f, f ^ 1) for f in range(BANDS)])]
    unnamed x4 -> x6, local copies, waits for them, and re-layouts: 0.68 us -> 1.6 us
    select_n x0 -> x1, other arithmetic: none -> 0.68 us  [pool(): jnp.where(jnp.arange(SLOTS, dtype=jnp.int32) < tile_count[0], tile_place,...]
    pallas_call x1, Pallas kernels: 2.83 us -> 2.14 us  [pool(): pl.pallas_call(pool_kernel, out_shape=(jax.ShapeDtypeStruct((PAIRS * BLOC...]
  transfers between devices with their start and end apart: 1 -> 1, of which waited for: 1 -> 0; matrix products, arithmetic and copies ran while one was open for 0% -> 0% of each run, Pallas kernels for 0% -> 2%
where the time goes in v4:
time: 67.6 us; the launch traced here: 67.4 us
  blocking collectives  46.6 us (69%)
  Pallas kernels  14.7 us (22%)
  starting transfers between devices  2.94 us (4%)
  local copies, waits for them, and re-layouts  1.6 us (2%)
  between operations  0.86 us (1%)
  other arithmetic  0.68 us (1%)
    all_to_all x2, blocking collectives, exchange(): lax.all_to_all(x, ('fft', 'tiles'), split_axis=0, concat_axis=0, axis_ind...  46.6 us
    pallas_call x1, Pallas kernels, conv(): pl.pallas_call(conv_kernel, out_shape=jax.ShapeDtypeStruct((BANDS * BLOCK...  9.3 us
    ppermute x1, starting transfers between devices, local(): pair = lax.ppermute(near, 'fft', [(f, f ^ 1) for f in range(BANDS)])  2.94 us
    pallas_call x1, Pallas kernels, pool(): pl.pallas_call(pool_kernel, out_shape=(jax.ShapeDtypeStruct((PAIRS * BLOC...  2.14 us
    pallas_call x1, Pallas kernels, spread(): pl.pallas_call(spread_kernel, out_shape=jax.ShapeDtypeStruct((SLOTS, 4096...  1.87 us
    unnamed x6, local copies, waits for them, and re-layouts  1.6 us
    pallas_call x1, Pallas kernels, first(): pl.pallas_call(first_kernel, out_shape=(jax.ShapeDtypeStruct((2, ROWS, 10...  1.35 us
  transfers between devices with their start and end apart: 1, of which 0 were waited for; matrix products, arithmetic and copies ran while one was open for 0% of the time, Pallas kernels for 2%

profile of v4, /device:TPU:1, one launch (start us, length us, event | category | flops | bytes accessed | tf_op | source)
XLA Modules:
  0.0 67.4 jit_solution(17118466373599543354)
XLA Ops:
  0.7 0.7 %compare_select_fusion = s32[256]{0:T(256)S(1)} fusion(s32[256]{0:T(256)} %param.11, s32[]{:T(128)} %bitcast.8), kind=kLoop, calls=%fused_computation | loop fusion | flops 512 | bytes 2052 | tf_op jit(solution)/shard_map/jit(_where)/select_n | solution.py:176
  1.3 0.0 copy-start.1
  1.3 1.6 %copy-done.1 = bf16[256,4096]{1,0:T(8,128)(2,1)S(1)} copy-done((bf16[256,4096]{1,0:T(8,128)(2,1)S(1)}, bf16[256,4096]{1,0:T(8,128)(2,1)}, u32[]{:S(2)}) %copy-start.1) | copy-done | bytes 2097176
  2.9 2.1 %pool.1 = (f32[512,128]{1,0:T(8,128)S(1)}, s32[256,128]{1,0:T(8,128)S(1)}) custom-call(s32[1,256]{1,0:T(1,128)S(1)} %bitcast.14, bf16[256,4096]{1,0:T(8,128)(2,1)S(1)} %copy-done.1), custom_call_target="tpu_custom_call" | custom-call | tf_op jit(solution)/shard_map/pool/pallas_call | solution.py:177
  5.1 28.7 %all_to_all.16 = f32[128,4,128]{2,1,0:T(4,128)S(1)} all-to-all(f32[128,4,128]{2,1,0:T(4,128)S(1)} %bitcast.13), channel_id=1, replica_groups={{0,8,16,24,32,40,48,56,64,72,80,88,96,104,112,120,128,136,144,152,160,1..., dimensions={0} | all-to-all | bytes 524288 | tf_op jit(solution)/shard_map/all_to_all | solution.py:498
  33.8 0.0 copy-start
  33.8 2.9 %collective-permute-start = (f32[512,128]{1,0:T(8,128)S(1)}, f32[512,128]{1,0:T(8,128)S(1)}, u32[]{:S(2)}, u32[]{:S(2)}) collective-permute-start(f32[512,128]{1,0:T(8,128)S(1)} %bitcast.11), channel_id=1, source_target_pairs={{0,1},{1,0},{2,3},{3,2},{4,5},{5,4},{6,7},{7,6},{8,9},{9,8},{10,11... | collective-permute-start | bytes 786440 | tf_op jit(solution)/shard_map/ppermute | solution.py:507
  36.7 1.4 %first.1 = (bf16[2,512,1024]{2,1,0:T(8,128)(2,1)S(1)}, s32[4,8,256]{2,1,0:T(8,128)S(1)}) custom-call(f32[512,128]{1,0:T(8,128)S(1)} %bitcast.12), custom_call_target="tpu_custom_call" | custom-call | flops 2000000000 | bytes 4000000 | tf_op jit(solution)/shard_map/first/pallas_call | solution.py:277
  38.1 0.0 collective-permute-done.pair_ref
  38.1 0.0 copy-done
  38.1 0.0 copy-start.2
  38.1 9.3 %conv.1 = f32[256,128]{1,0:T(8,128)S(1)} custom-call(bf16[2,512,1024]{2,1,0:T(8,128)(2,1)S(1)} %get-tuple-element.11.planes_ref, s32[4,8,256]{2,1,0:T(8,128)S(1)} %get-tuple-element.12.codes_ref, f32[512,128]{1,0:T(8,128)S(1)} %collective-permute-done.pair_ref, bf16[8,4,1024,256]{3,2,1,0:T(8,128)(2,1)} %constant.10.clone.fwd_hbm, ...), custom_call_target="tpu_custom_call" | custom-call | tf_op jit(solution)/shard_map/conv/pallas_call | solution.py:421
  47.4 17.9 %all_to_all.17 = f32[256,1,128]{2,1,0:T(1,128)S(1)} all-to-all(f32[256,1,128]{2,1,0:T(1,128)S(1)} %bitcast.9), channel_id=1, replica_groups=mesh['tiles'=32,'fft'=8] {'fft','tiles'}, dimensions={0} | all-to-all | bytes 262144 | tf_op jit(solution)/shard_map/all_to_all | solution.py:498
  65.4 0.0 copy-done.2
  65.4 1.9 %spread.1 = bf16[256,4096]{1,0:T(8,128)(2,1)} custom-call(s32[256,128]{1,0:T(8,128)S(1)} %get-tuple-element.9.meta_ref, f32[256,128]{1,0:T(8,128)S(1)} %bitcast.10, bf16[256,4096]{1,0:T(8,128)(2,1)S(1)} %copy-done.2), custom_call_target="tpu_custom_call" | custom-call | tf_op jit(solution)/shard_map/spread/pallas_call | solution.py:486
Async XLA Ops:
  1.3 1.6 %copy-start.1 = (bf16[256,4096]{1,0:T(8,128)(2,1)S(1)}, bf16[256,4096]{1,0:T(8,128)(2,1)}, u32[]{:S(2)}) copy-start(bf16[256,4096]{1,0:T(8,128)(2,1)} %cot_hbm.1) | copy-start | bytes 6291460
  33.8 4.3 %copy-start = (f32[2,1536,256]{2,1,0:T(8,128)S(1)}, f32[2,1536,256]{2,1,0:T(8,128)}, u32[]{:S(2)}) copy-start(f32[2,1536,256]{2,1,0:T(8,128)} %psf_hbm.1) | copy-start | bytes 9437188
  33.8 4.3 %collective-permute-start = (f32[512,128]{1,0:T(8,128)S(1)}, f32[512,128]{1,0:T(8,128)S(1)}, u32[]{:S(2)}, u32[]{:S(2)}) collective-permute-start(f32[512,128]{1,0:T(8,128)S(1)} %bitcast.11), channel_id=1, source_target_pairs={{0,1},{1,0},{2,3},{3,2},{4,5},{5,4},{6,7},{7,6},{8,9},{9,8},{10,11... | collective-permute-start | bytes 786440 | tf_op jit(solution)/shard_map/ppermute | solution.py:507
  38.1 27.3 %copy-start.2 = (bf16[256,4096]{1,0:T(8,128)(2,1)S(1)}, bf16[256,4096]{1,0:T(8,128)(2,1)}, u32[]{:S(2)}) copy-start(bf16[256,4096]{1,0:T(8,128)(2,1)} %base_ref.1) | copy-start | bytes 6291460

commit v5 on v4

--- a/solution.py
+++ b/solution.py
@@ -30,7 +30,8 @@
 PAIRS = BANDS // 2
 BF = jnp.bfloat16
 F32 = jnp.float32
-VMEM_LIMIT = 48 * 1024 * 1024
+VMEM_LIMIT = 52 * 1024 * 1024
+CONV_VMEM_LIMIT = 48 * 1024 * 1024
 
 
 def split_np(table):
@@ -443,7 +444,7 @@
             pltpu.VMEM((2, PAIRS, CELLS, 256), F32),
             pltpu.SemaphoreType.DMA((5,)),
         ],
-        compiler_params=pltpu.CompilerParams(vmem_limit_bytes=VMEM_LIMIT),
+        compiler_params=pltpu.CompilerParams(vmem_limit_bytes=CONV_VMEM_LIMIT),
         name="conv",
     )(planes, codes, pair, jnp.asarray(fwd), jnp.asarray(rfwd), psf, jnp.asarray(rback), jnp.asarray(back))
 

time: 67.6 us -> 66.7 us (0.987)
  local copies, waits for them, and re-layouts: 1.6 us -> 0.01 us
    unnamed x6 -> x4, local copies, waits for them, and re-layouts: 1.6 us -> 0.01 us
where the time goes in v5:
time: 66.7 us; the launch traced here: 66.5 us
  blocking collectives  46.6 us (70%)
  Pallas kernels  15.3 us (23%)
  starting transfers between devices  2.93 us (4%)
  between operations  0.86 us (1%)
  other arithmetic  0.68 us (1%)
    all_to_all x2, blocking collectives, exchange(): lax.all_to_all(x, ('fft', 'tiles'), split_axis=0, concat_axis=0, axis_ind...  46.6 us
    pallas_call x1, Pallas kernels, conv(): pl.pallas_call(conv_kernel, out_shape=jax.ShapeDtypeStruct((BANDS * BLOCK...  9.31 us
    ppermute x1, starting transfers between devices, local(): pair = lax.ppermute(near, 'fft', [(f, f ^ 1) for f in range(BANDS)])  2.93 us
    pallas_call x1, Pallas kernels, pool(): pl.pallas_call(pool_kernel, out_shape=(jax.ShapeDtypeStruct((PAIRS * BLOC...  2.82 us
    pallas_call x1, Pallas kernels, spread(): pl.pallas_call(spread_kernel, out_shape=jax.ShapeDtypeStruct((SLOTS, 4096...  1.87 us
    pallas_call x1, Pallas kernels, first(): pl.pallas_call(first_kernel, out_shape=(jax.ShapeDtypeStruct((2, ROWS, 10...  1.35 us
  transfers between devices with their start and end apart: 1, of which 0 were waited for; matrix products, arithmetic and copies ran while one was open for 0% of the time, Pallas kernels for 2%

profile of v5, /device:TPU:1, one launch (start us, length us, event | category | flops | bytes accessed | tf_op | source)
XLA Modules:
  0.0 66.5 jit_solution(3063678563209242241)
XLA Ops:
  0.7 0.7 %compare_select_fusion = s32[256]{0:T(256)S(1)} fusion(s32[256]{0:T(256)} %param.11, s32[]{:T(128)} %bitcast.8), kind=kLoop, calls=%fused_computation | loop fusion | flops 512 | bytes 2052 | tf_op jit(solution)/shard_map/jit(_where)/select_n | solution.py:177
  1.3 2.8 %pool.1 = (f32[512,128]{1,0:T(8,128)S(1)}, s32[256,128]{1,0:T(8,128)S(1)}) custom-call(s32[1,256]{1,0:T(1,128)S(1)} %bitcast.14, bf16[256,4096]{1,0:T(8,128)(2,1)} %cot_hbm.1), custom_call_target="tpu_custom_call" | custom-call | tf_op jit(solution)/shard_map/pool/pallas_call | solution.py:178
  4.2 28.7 %all_to_all.16 = f32[128,4,128]{2,1,0:T(4,128)S(1)} all-to-all(f32[128,4,128]{2,1,0:T(4,128)S(1)} %bitcast.13), channel_id=1, replica_groups={{0,8,16,24,32,40,48,56,64,72,80,88,96,104,112,120,128,136,144,152,160,1..., dimensions={0} | all-to-all | bytes 524288 | tf_op jit(solution)/shard_map/all_to_all | solution.py:499
  32.9 0.0 copy-start
  32.9 2.9 %collective-permute-start = (f32[512,128]{1,0:T(8,128)S(1)}, f32[512,128]{1,0:T(8,128)S(1)}, u32[]{:S(2)}, u32[]{:S(2)}) collective-permute-start(f32[512,128]{1,0:T(8,128)S(1)} %bitcast.11), channel_id=1, source_target_pairs={{0,1},{1,0},{2,3},{3,2},{4,5},{5,4},{6,7},{7,6},{8,9},{9,8},{10,11... | collective-permute-start | bytes 786440 | tf_op jit(solution)/shard_map/ppermute | solution.py:508
  35.8 1.4 %first.1 = (bf16[2,512,1024]{2,1,0:T(8,128)(2,1)S(1)}, s32[4,8,256]{2,1,0:T(8,128)S(1)}) custom-call(f32[512,128]{1,0:T(8,128)S(1)} %bitcast.12), custom_call_target="tpu_custom_call" | custom-call | flops 2000000000 | bytes 4000000 | tf_op jit(solution)/shard_map/first/pallas_call | solution.py:278
  37.2 0.0 collective-permute-done.pair_ref
  37.2 0.0 copy-done
  37.2 0.0 copy-start.1
  37.2 9.3 %conv.1 = f32[256,128]{1,0:T(8,128)S(1)} custom-call(bf16[2,512,1024]{2,1,0:T(8,128)(2,1)S(1)} %get-tuple-element.11.planes_ref, s32[4,8,256]{2,1,0:T(8,128)S(1)} %get-tuple-element.12.codes_ref, f32[512,128]{1,0:T(8,128)S(1)} %collective-permute-done.pair_ref, bf16[8,4,1024,256]{3,2,1,0:T(8,128)(2,1)} %constant.10.clone.fwd_hbm, ...), custom_call_target="tpu_custom_call" | custom-call | tf_op jit(solution)/shard_map/conv/pallas_call | solution.py:422
  46.5 17.9 %all_to_all.17 = f32[256,1,128]{2,1,0:T(1,128)S(1)} all-to-all(f32[256,1,128]{2,1,0:T(1,128)S(1)} %bitcast.9), channel_id=1, replica_groups=mesh['tiles'=32,'fft'=8] {'fft','tiles'}, dimensions={0} | all-to-all | bytes 262144 | tf_op jit(solution)/shard_map/all_to_all | solution.py:499
  64.5 0.0 copy-done.1
  64.5 1.9 %spread.1 = bf16[256,4096]{1,0:T(8,128)(2,1)} custom-call(s32[256,128]{1,0:T(8,128)S(1)} %get-tuple-element.9.meta_ref, f32[256,128]{1,0:T(8,128)S(1)} %bitcast.10, bf16[256,4096]{1,0:T(8,128)(2,1)S(1)} %copy-done.1), custom_call_target="tpu_custom_call" | custom-call | tf_op jit(solution)/shard_map/spread/pallas_call | solution.py:487
Async XLA Ops:
  32.9 4.3 %copy-start = (f32[2,1536,256]{2,1,0:T(8,128)S(1)}, f32[2,1536,256]{2,1,0:T(8,128)}, u32[]{:S(2)}) copy-start(f32[2,1536,256]{2,1,0:T(8,128)} %psf_hbm.1) | copy-start | bytes 9437188
  32.9 4.3 %collective-permute-start = (f32[512,128]{1,0:T(8,128)S(1)}, f32[512,128]{1,0:T(8,128)S(1)}, u32[]{:S(2)}, u32[]{:S(2)}) collective-permute-start(f32[512,128]{1,0:T(8,128)S(1)} %bitcast.11), channel_id=1, source_target_pairs={{0,1},{1,0},{2,3},{3,2},{4,5},{5,4},{6,7},{7,6},{8,9},{9,8},{10,11... | collective-permute-start | bytes 786440 | tf_op jit(solution)/shard_map/ppermute | solution.py:508
  37.2 27.3 %copy-start.1 = (bf16[256,4096]{1,0:T(8,128)(2,1)S(1)}, bf16[256,4096]{1,0:T(8,128)(2,1)}, u32[]{:S(2)}) copy-start(bf16[256,4096]{1,0:T(8,128)(2,1)} %base_ref.1) | copy-start | bytes 6291460

commit v6 on v5

--- a/solution.py
+++ b/solution.py
@@ -31,7 +31,7 @@
 BF = jnp.bfloat16
 F32 = jnp.float32
 VMEM_LIMIT = 52 * 1024 * 1024
-CONV_VMEM_LIMIT = 48 * 1024 * 1024
+CONV_VMEM_LIMIT = 47 * 1024 * 1024
 
 
 def split_np(table):
@@ -230,7 +230,7 @@
     return jnp.where(hit, jnp.ones((), BF), jnp.zeros((), BF))
 
 
-def scatter(tv, tm, planes):
+def scatter(tv, tm, planes, hots):
     row16 = iota((16, 256), 0)
 
     def one(x, carry):
@@ -250,6 +250,8 @@
                 ]
                 sides.append(jnp.concatenate(parts, axis=0))
             hot = hot_of(code, 256 if nbr == 0 else 128)
+            if nbr == 0:
+                hots[x] = hot
             outs.append(dot_nt(jnp.concatenate(sides, axis=1), jnp.concatenate([hot, hot], axis=1)))
         near_r, near_l = outs[0][:, :128], outs[0][:, 128:]
         far_l, far_r = outs[1], outs[2]
@@ -267,10 +269,10 @@
     lax.fori_loop(0, PAIRS, one, 0, unroll=PAIRS)
 
 
-def first_kernel(near_ref, planes_ref, codes_ref, tv, tm):
+def first_kernel(near_ref, planes_ref, codes_ref, hots_ref, tv, tm):
     arrive(near_ref, tv, tm)
     codes_ref[...] = tm[:, 0]
-    scatter(tv, tm, planes_ref)
+    scatter(tv, tm, planes_ref, hots_ref)
 
 
 def first(near):
@@ -280,9 +282,10 @@
         out_shape=(
             jax.ShapeDtypeStruct((2, ROWS, 1024), BF),
             jax.ShapeDtypeStruct((PAIRS, 8, 256), jnp.int32),
+            jax.ShapeDtypeStruct((PAIRS, 256, 256), BF),
         ),
         in_specs=[vmem_spec],
-        out_specs=(vmem_spec, vmem_spec),
+        out_specs=(vmem_spec, vmem_spec, vmem_spec),
         scratch_shapes=[
             pltpu.VMEM((PAIRS, 3, CELLS, 256), F32),
             pltpu.VMEM((PAIRS, 3, 8, 256), jnp.int32),
@@ -294,8 +297,8 @@
 
 
 def conv_kernel(
-    planes_ref, codes_ref, pair_ref, fwd_hbm, rfwd_hbm, psf_hbm, rback_hbm, back_hbm, out_ref,
-    fwd, rfwd, psf, rback, back, tv, tm, planes, y_s, g_s, q_s, z_s, s_s, tg, sems,
+    planes_ref, codes_ref, hots_ref, pair_ref, fwd_hbm, rfwd_hbm, psf_hbm, rback_hbm, back_hbm, out_ref,
+    fwd, rfwd, psf, rback, back, tv, tm, planes, hots, y_s, g_s, q_s, z_s, s_s, tg, sems,
 ):
     f = lax.axis_index("fft")
     core = f & 1
@@ -310,7 +313,7 @@
     arrive(pair_ref, tv, tm)
     copies[1].start()
     copies[2].start()
-    scatter(tv, tm, planes)
+    scatter(tv, tm, planes, hots)
     copies[3].start()
     copies[4].start()
 
@@ -386,7 +389,7 @@
         def gather(x, carry, half=half):
             base = pl.multiple_of(half * 64 + x * 16, 16)
             code = codes_ref[x] if half == 0 else tm[x, 0]
-            hot = hot_of(code, 256)
+            hot = hots_ref[x] if half == 0 else hots[x]
             mask = row16 == jnp.broadcast_to(code[0:1, :] >> 8, (16, 256))
             left = [
                 jnp.concatenate(
@@ -415,7 +418,7 @@
             out_ref[pl.ds(base, BLOCKS), :] = turned[x * BLOCKS : (x + 1) * BLOCKS, :]
 
 
-def conv(planes, codes, pair, psf):
+def conv(planes, codes, hots, pair, psf):
     fwd, back, rfwd, rback = tables()
     any_spec = pl.BlockSpec(memory_space=pl.ANY)
     vmem_spec = pl.BlockSpec(memory_space=pltpu.VMEM)
@@ -423,7 +426,7 @@
         conv_kernel,
         out_shape=jax.ShapeDtypeStruct((BANDS * BLOCKS, 128), F32),
         in_specs=[
-            vmem_spec, vmem_spec, vmem_spec,
+            vmem_spec, vmem_spec, vmem_spec, vmem_spec,
             any_spec, any_spec, any_spec, any_spec, any_spec,
         ],
         out_specs=vmem_spec,
@@ -436,6 +439,7 @@
             pltpu.VMEM((PAIRS, 3, CELLS, 256), F32),
             pltpu.VMEM((PAIRS, 3, 8, 256), jnp.int32),
             pltpu.VMEM((2, ROWS, 1024), BF),
+            pltpu.VMEM((PAIRS, 256, 256), BF),
             pltpu.VMEM((2, 4, 256, STRIP), BF),
             pltpu.VMEM((CHUNKS, 4, 2 * STEP, STRIP), F32),
             pltpu.VMEM((2, 4, 2 * PART0, STRIP), BF),
@@ -446,7 +450,7 @@
         ],
         compiler_params=pltpu.CompilerParams(vmem_limit_bytes=CONV_VMEM_LIMIT),
         name="conv",
-    )(planes, codes, pair, jnp.asarray(fwd), jnp.asarray(rfwd), psf, jnp.asarray(rback), jnp.asarray(back))
+    )(planes, codes, hots, pair, jnp.asarray(fwd), jnp.asarray(rfwd), psf, jnp.asarray(rback), jnp.asarray(back))
 
 
 def spread_kernel(meta_ref, back_ref, base_ref, out_hbm, done, sems):
@@ -506,8 +510,8 @@
     groups = [[f * BLOCKS + t for f in range(c, BANDS, 2) for t in range(BLOCKS)] for c in range(2)]
     near = exchange(message.reshape(PAIRS * BLOCKS, 4, 128), groups).reshape(-1, 128)
     pair = lax.ppermute(near, "fft", [(f, f ^ 1) for f in range(BANDS)])
-    planes, codes = first(near)
-    partial = conv(planes, codes, pair, psf_spectrum)
+    planes, codes, hots = first(near)
+    partial = conv(planes, codes, hots, pair, psf_spectrum)
     returned = exchange(partial)
     return spread(meta, returned, base_grad)
 

time: 66.7 us -> 66.6 us (level)
  no operation moved by 1% of the time
where the time goes in v6:
time: 66.6 us; the launch traced here: 66.4 us
  blocking collectives  46.6 us (70%)
  Pallas kernels  15.3 us (23%)
  starting transfers between devices  2.93 us (4%)
  between operations  0.86 us (1%)
  other arithmetic  0.68 us (1%)
    all_to_all x2, blocking collectives, exchange(): lax.all_to_all(x, ('fft', 'tiles'), split_axis=0, concat_axis=0, axis_ind...  46.6 us
    pallas_call x1, Pallas kernels, conv(): pl.pallas_call(conv_kernel, out_shape=jax.ShapeDtypeStruct((BANDS * BLOCK...  9.24 us
    ppermute x1, starting transfers between devices, local(): pair = lax.ppermute(near, 'fft', [(f, f ^ 1) for f in range(BANDS)])  2.93 us
    pallas_call x1, Pallas kernels, pool(): pl.pallas_call(pool_kernel, out_shape=(jax.ShapeDtypeStruct((PAIRS * BLOC...  2.82 us
    pallas_call x1, Pallas kernels, spread(): pl.pallas_call(spread_kernel, out_shape=jax.ShapeDtypeStruct((SLOTS, 4096...  1.87 us
    pallas_call x1, Pallas kernels, first(): pl.pallas_call(first_kernel, out_shape=(jax.ShapeDtypeStruct((2, ROWS, 10...  1.38 us
  transfers between devices with their start and end apart: 1, of which 0 were waited for; matrix products, arithmetic and copies ran while one was open for 0% of the time, Pallas kernels for 2%

profile of v6, /device:TPU:1, one launch (start us, length us, event | category | flops | bytes accessed | tf_op | source)
XLA Modules:
  0.0 66.4 jit_solution(16133588965571734231)
XLA Ops:
  0.7 0.7 %compare_select_fusion = s32[256]{0:T(256)S(1)} fusion(s32[256]{0:T(256)} %param.11, s32[]{:T(128)} %bitcast.8), kind=kLoop, calls=%fused_computation | loop fusion | flops 512 | bytes 2052 | tf_op jit(solution)/shard_map/jit(_where)/select_n | solution.py:177
  1.3 2.8 %pool.1 = (f32[512,128]{1,0:T(8,128)S(1)}, s32[256,128]{1,0:T(8,128)S(1)}) custom-call(s32[1,256]{1,0:T(1,128)S(1)} %bitcast.14, bf16[256,4096]{1,0:T(8,128)(2,1)} %cot_hbm.1), custom_call_target="tpu_custom_call" | custom-call | tf_op jit(solution)/shard_map/pool/pallas_call | solution.py:178
  4.2 28.7 %all_to_all.16 = f32[128,4,128]{2,1,0:T(4,128)S(1)} all-to-all(f32[128,4,128]{2,1,0:T(4,128)S(1)} %bitcast.13), channel_id=1, replica_groups={{0,8,16,24,32,40,48,56,64,72,80,88,96,104,112,120,128,136,144,152,160,1..., dimensions={0} | all-to-all | bytes 524288 | tf_op jit(solution)/shard_map/all_to_all | solution.py:503
  32.9 0.0 copy-start
  32.9 2.9 %collective-permute-start = (f32[512,128]{1,0:T(8,128)S(1)}, f32[512,128]{1,0:T(8,128)S(1)}, u32[]{:S(2)}, u32[]{:S(2)}) collective-permute-start(f32[512,128]{1,0:T(8,128)S(1)} %bitcast.11), channel_id=1, source_target_pairs={{0,1},{1,0},{2,3},{3,2},{4,5},{5,4},{6,7},{7,6},{8,9},{9,8},{10,11... | collective-permute-start | bytes 786440 | tf_op jit(solution)/shard_map/ppermute | solution.py:512
  35.8 1.4 %first.1 = (bf16[2,512,1024]{2,1,0:T(8,128)(2,1)S(1)}, s32[4,8,256]{2,1,0:T(8,128)S(1)}, bf16[4,256,256]{2,1,0:T(8,128)(2,1)S(1)}) custom-call(f32[512,128]{1,0:T(8,128)S(1)} %bitcast.12), custom_call_target="tpu_custom_call" | custom-call | flops 2000000000 | bytes 4000000 | tf_op jit(solution)/shard_map/first/pallas_call | solution.py:280
  37.2 0.0 collective-permute-done.pair_ref
  37.2 0.0 copy-done
  37.2 0.0 copy-start.1
  37.2 9.2 %conv.1 = f32[256,128]{1,0:T(8,128)S(1)} custom-call(bf16[2,512,1024]{2,1,0:T(8,128)(2,1)S(1)} %get-tuple-element.12.planes_ref, s32[4,8,256]{2,1,0:T(8,128)S(1)} %get-tuple-element.13.codes_ref, bf16[4,256,256]{2,1,0:T(8,128)(2,1)S(1)} %get-tuple-element.14.hots_ref, f32[512,128]{1,0:T(8,128)S(1)} %collective-permute-done.pair_ref, ...), custom_call_target="tpu_custom_call" | custom-call | tf_op jit(solution)/shard_map/conv/pallas_call | solution.py:425
  46.5 17.9 %all_to_all.17 = f32[256,1,128]{2,1,0:T(1,128)S(1)} all-to-all(f32[256,1,128]{2,1,0:T(1,128)S(1)} %bitcast.9), channel_id=1, replica_groups=mesh['tiles'=32,'fft'=8] {'fft','tiles'}, dimensions={0} | all-to-all | bytes 262144 | tf_op jit(solution)/shard_map/all_to_all | solution.py:503
  64.4 0.0 copy-done.1
  64.4 1.9 %spread.1 = bf16[256,4096]{1,0:T(8,128)(2,1)} custom-call(s32[256,128]{1,0:T(8,128)S(1)} %get-tuple-element.10.meta_ref, f32[256,128]{1,0:T(8,128)S(1)} %bitcast.10, bf16[256,4096]{1,0:T(8,128)(2,1)S(1)} %copy-done.1), custom_call_target="tpu_custom_call" | custom-call | tf_op jit(solution)/shard_map/spread/pallas_call | solution.py:491
Async XLA Ops:
  32.9 4.3 %copy-start = (f32[2,1536,256]{2,1,0:T(8,128)S(1)}, f32[2,1536,256]{2,1,0:T(8,128)}, u32[]{:S(2)}) copy-start(f32[2,1536,256]{2,1,0:T(8,128)} %psf_hbm.1) | copy-start | bytes 9437188
  32.9 4.3 %collective-permute-start = (f32[512,128]{1,0:T(8,128)S(1)}, f32[512,128]{1,0:T(8,128)S(1)}, u32[]{:S(2)}, u32[]{:S(2)}) collective-permute-start(f32[512,128]{1,0:T(8,128)S(1)} %bitcast.11), channel_id=1, source_target_pairs={{0,1},{1,0},{2,3},{3,2},{4,5},{5,4},{6,7},{7,6},{8,9},{9,8},{10,11... | collective-permute-start | bytes 786440 | tf_op jit(solution)/shard_map/ppermute | solution.py:512
  37.2 27.2 %copy-start.1 = (bf16[256,4096]{1,0:T(8,128)(2,1)S(1)}, bf16[256,4096]{1,0:T(8,128)(2,1)}, u32[]{:S(2)}) copy-start(bf16[256,4096]{1,0:T(8,128)(2,1)} %base_ref.1) | copy-start | bytes 6291460
